TPU v7x, 256 devices: a whole 4x4x8 slice. The times are simulated.
256 devices in a mesh: expert: 64 (over y, z, core), dp: 4 (over x).
Axes of the slice: x: 4, y: 4, z: 8, core: 2. Of those that a mesh axis runs over, the one named last changes fastest.
Arguments:
- tokens: bfloat16 [32768, 2048], P(('expert', 'dp')), may hold values from -6 to 6
- out_grad: bfloat16 [32768, 2048], P(('expert', 'dp')), may hold values from -6 to 6
- expert_ids: int32 [32768, 8], P(('expert', 'dp')), may hold values from 0 to 63, all different within a row; in each aligned block of 128 rows (0 to 127, 128 to 255, ...) at most 17 rows name the same one
- route_probs: bfloat16 [32768, 8], P(('expert', 'dp')), may hold values from 0.049804688 to 0.5
- w_gate_up: bfloat16 [64, 2048, 768], P('expert'), may hold values from -0.125 to 0.125
- w_down: bfloat16 [64, 2048, 384], P('expert'), may hold values from -0.3125 to 0.3125
Outputs:
- token_grad: bfloat16 [32768, 2048], P(('expert', 'dp'))
- prob_grad: bfloat16 [32768, 8], P(('expert', 'dp'))
- grad_gate_up: float32 [64, 2048, 768], P('expert', 'dp')
- grad_down: float32 [64, 2048, 384], P('expert', 'dp')
Inputs may be any that keep to these rules, and one draw needn't show every extreme that they name: `expert_ids`: among the 128 tokens of one device (aligned blocks of rows) no expert is named by more than 17 tokens, a bound that some block reaches; a token names 8 different experts.
All inputs are finite; a program needn't handle non-finite values.
Results may differ from a plain program's by a relative error of at most 0.014.
Values may be sent and summed in bfloat16 or wider, within the bound.
A program may use at most 128 MiB of HBM per device.

v0:
```python
import jax
import jax.numpy as jnp
from jax import lax
from jax.sharding import PartitionSpec as P


def contract_rows(left, right):
    return lax.dot_general(
        left, right, (((0,), (0,)), ((), ())), preferred_element_type=jnp.float32
    )


def contract_cols(left, right):
    return lax.dot_general(
        left, right, (((1,), (1,)), ((), ())), preferred_element_type=jnp.float32
    )


def on_device(tokens, out_grad, expert_ids, route_probs, w_gate_up, w_down):
    tok_rows, width = tokens.shape
    per_token = expert_ids.shape[1]
    expert_count = lax.axis_size("expert")
    hidden_units = w_down.shape[2]
    capacity = min(tok_rows, max(2, 17 * tok_rows * per_token // (16 * expert_count)))
    route_count = tok_rows * per_token
    slot_total = expert_count * capacity
    flat_ids = expert_ids.reshape(route_count)
    onehot = (flat_ids[:, None] == jnp.arange(expert_count, dtype=jnp.int32)[None, :]).astype(
        jnp.int32
    )
    slot_rank = jnp.sum((jnp.cumsum(onehot, axis=0) - 1) * onehot, axis=1)
    slot_index = flat_ids * capacity + slot_rank
    source_route = (
        jnp.zeros((slot_total,), jnp.int32)
        .at[slot_index]
        .set(jnp.arange(route_count, dtype=jnp.int32) + 1)
    )
    live_mask = source_route > 0
    route_pick = jnp.maximum(source_route - 1, 0)
    token_pick = route_pick // per_token
    zero_bf = jnp.zeros((), jnp.bfloat16)
    send_tokens = jnp.where(live_mask[:, None], tokens[token_pick], zero_bf).reshape(
        expert_count, capacity, width
    )
    send_grads = jnp.where(live_mask[:, None], out_grad[token_pick], zero_bf).reshape(
        expert_count, capacity, width
    )
    send_probs = jnp.where(
        live_mask, route_probs.reshape(route_count)[route_pick], zero_bf
    ).reshape(expert_count, capacity)
    recv_tokens, recv_grads, recv_probs = (
        lax.all_to_all(send_tokens, "expert", split_axis=0, concat_axis=0, tiled=True),
        lax.all_to_all(send_grads, "expert", split_axis=0, concat_axis=0, tiled=True),
        lax.all_to_all(send_probs, "expert", split_axis=0, concat_axis=0, tiled=True),
    )
    x_in = recv_tokens.reshape(slot_total, width)
    dy_in = recv_grads.reshape(slot_total, width)
    p_in = recv_probs.reshape(slot_total)
    weight_gu = w_gate_up[0]
    weight_dn = w_down[0]
    gate_up = jnp.dot(x_in, weight_gu, preferred_element_type=jnp.float32)
    gate_val = gate_up[:, :hidden_units]
    up_val = gate_up[:, hidden_units:]
    sigmoid_gate = jax.nn.sigmoid(gate_val)
    silu_gate = gate_val * sigmoid_gate
    hidden_act = (silu_gate * up_val).astype(jnp.bfloat16)
    expert_out = contract_cols(hidden_act, weight_dn)
    prob_slot = jnp.sum(dy_in.astype(jnp.float32) * expert_out, axis=1).astype(jnp.bfloat16)
    scaled_grad = (p_in.astype(jnp.float32)[:, None] * dy_in.astype(jnp.float32)).astype(
        jnp.bfloat16
    )
    hidden_grad = jnp.dot(scaled_grad, weight_dn, preferred_element_type=jnp.float32)
    gate_grad = hidden_grad * up_val * sigmoid_gate * (1.0 + gate_val * (1.0 - sigmoid_gate))
    up_grad = hidden_grad * silu_gate
    gate_up_grad = jnp.concatenate([gate_grad, up_grad], axis=1).astype(jnp.bfloat16)
    route_grad = contract_cols(gate_up_grad, weight_gu).astype(jnp.bfloat16)
    back_grad, back_prob = (
        lax.all_to_all(
            route_grad.reshape(expert_count, capacity, width),
            "expert",
            split_axis=0,
            concat_axis=0,
            tiled=True,
        ),
        lax.all_to_all(
            prob_slot.reshape(expert_count, capacity),
            "expert",
            split_axis=0,
            concat_axis=0,
            tiled=True,
        ),
    )
    routed_rows = back_grad.reshape(slot_total, width)[slot_index].reshape(
        tok_rows, per_token, width
    )
    token_grad = jnp.sum(routed_rows.astype(jnp.float32), axis=1).astype(jnp.bfloat16)
    prob_grad = back_prob.reshape(slot_total)[slot_index].reshape(tok_rows, per_token)
    summed = lax.psum_scatter(
        jnp.concatenate(
            [contract_rows(x_in, gate_up_grad), contract_rows(scaled_grad, hidden_act)], axis=1
        ).astype(jnp.bfloat16),
        "dp",
        scatter_dimension=0,
        tiled=True,
    ).astype(jnp.float32)
    grad_gate_up = summed[None, :, : 2 * hidden_units]
    grad_down = summed[None, :, 2 * hidden_units :]
    return (token_grad, prob_grad, grad_gate_up, grad_down)


def solution(mesh):
    in_specs = (
        P(("expert", "dp"), None),
        P(("expert", "dp"), None),
        P(("expert", "dp"), None),
        P(("expert", "dp"), None),
        P("expert", None, None),
        P("expert", None, None),
    )
    out_specs = (
        P(("expert", "dp"), None),
        P(("expert", "dp"), None),
        P("expert", "dp", None),
        P("expert", "dp", None),
    )
    return jax.shard_map(
        on_device, mesh=mesh, in_specs=in_specs, out_specs=out_specs, check_vma=False
    )
```

profile of v0, /device:TPU:1, one launch (start us, length us, event | category | flops | bytes accessed | tf_op | source)
XLA Modules:
  0.0 675.4 jit_solution(14593063518181910211)
XLA Ops:
  9.7 31.1 %reduce-window.6 = s32[64,8,128]{2,1,0:T(8,128)S(1)} reduce-window(s32[64,8,128]{2,1,0:T(8,128)} %fusion.13, s32[]{:T(128)} %constant.34.clone.1), window={size=1x1x128 pad=0_0x0_0x127_0}, to_apply=%region_0.0 | reduce-window | flops 8323072 | bytes 524292 | tf_op jit(solution)/shard_map/reduce-window
  50.2 6.9 %gather_fusion = bf16[1088]{0:T(1024)(128)(2,1)S(1)} fusion(bf16[1024]{0:T(1024)(128)(2,1)S(1)} %reshape.133, s32[2048]{0:T(1024)S(1)} %get-tuple-element.26), kind=kCustom, calls=%fused_computation | custom fusion | bytes 8704 | tf_op jit(solution)/shard_map/gather | solution.py:49
  57.9 13.2 %all-to-all-start = ((bf16[64,1,17]{2,1,0:T(2,128)(2,1)}), bf16[64,1,17]{2,1,0:T(2,128)(2,1)S(1)}, u32[]{:S(2)}, u32[]{:S(2)}) async-start(bf16[64,1,17]{2,1,0:T(2,128)(2,1)} %all_to_all.25), calls=%async_computation | async-start | bytes 65536 | tf_op jit(solution)/shard_map/all_to_all | solution.py:54
  71.2 11.7 %gather_fusion.1 = bf16[1088,2048]{1,0:T(8,128)(2,1)} fusion(bf16[128,2048]{1,0:T(8,128)(2,1)} %param.7, s32[2048]{0:T(1024)S(1)} %get-tuple-element.25), kind=kCustom, calls=%fused_computation.1 | custom fusion | bytes 8917248 | tf_op jit(solution)/shard_map/gather | solution.py:45
  82.9 7.6 %gather.21 = bf16[64,17,2048]{2,1,0:T(8,128)(2,1)} reshape(bf16[1088,2048]{1,0:T(8,128)(2,1)} %gather_fusion.1) | data formatting | bytes 8912896 | tf_op jit(solution)/shard_map/gather | solution.py:45
  90.5 11.7 %gather_fusion.2 = bf16[1088,2048]{1,0:T(8,128)(2,1)} fusion(bf16[128,2048]{1,0:T(8,128)(2,1)} %param.6, s32[2048]{0:T(1024)S(1)} %get-tuple-element.25), kind=kCustom, calls=%fused_computation.2 | custom fusion | bytes 8917248 | tf_op jit(solution)/shard_map/gather | solution.py:42
  102.2 7.6 %gather.23 = bf16[64,17,2048]{2,1,0:T(8,128)(2,1)} reshape(bf16[1088,2048]{1,0:T(8,128)(2,1)} %gather_fusion.2) | data formatting | bytes 8912896 | tf_op jit(solution)/shard_map/gather | solution.py:42
  109.8 10.2 %broadcast_select_fusion = (bf16[64,17,2048]{2,1,0:T(8,128)(2,1)}, bf16[64,17,2048]{2,1,0:T(8,128)(2,1)}) fusion(bf16[64,17,2048]{2,1,0:T(8,128)(2,1)} %gather.23, pred[64,17]{1,0:T(8,128)(4,1)S(1)} %broadcast_in_dim.44, bf16[64,17,2048]{2,1,0:T(8,128)(2,1)} %gather.21), kind=kLoop, calls=%fused_computation.10 | loop fusion | flops 4456448 | bytes 17826880 | tf_op jit(solution)/shard_map/jit(_where)/select_n | solution.py:42
  120.0 151.6 %all_to_all.31 = bf16[64,17,2048]{2,1,0:T(8,128)(2,1)} all-to-all(bf16[64,17,2048]{2,1,0:T(8,128)(2,1)} %get-tuple-element.22), channel_id=1, replica_groups=mesh['expert'=64,'dp'=4] {'expert'}, dimensions={0} | all-to-all | bytes 8912896 | tf_op jit(solution)/shard_map/all_to_all | solution.py:53
  271.6 6.0 all-to-all-start.2
  277.9 6.5 multiply_convert_fusion
  284.4 7.7 %convert_element_type.71 = bf16[1088,2048]{1,0:T(8,128)(2,1)} reshape(bf16[64,17,2048]{2,1,0:T(8,128)(2,1)} %multiply_convert_fusion) | data formatting | bytes 8912896 | tf_op jit(solution)/shard_map/convert_element_type | solution.py:69
  292.1 126.3 %all-to-all-done.2 = bf16[64,17,2048]{2,1,0:T(8,128)(2,1)} async-done(((bf16[64,17,2048]{2,1,0:T(8,128)(2,1)}), bf16[64,17,2048]{2,1,0:T(8,128)(2,1)}, u32[]{:S(2)}, u32[]{:S(2)}) %all-to-all-start.2) | async-done | bytes 4456480 | tf_op jit(solution)/shard_map/all_to_all | solution.py:52
  418.4 7.8 %reshape.134 = bf16[1088,2048]{1,0:T(8,128)(2,1)} reshape(bf16[64,17,2048]{2,1,0:T(8,128)(2,1)} %all-to-all-done.2) | data formatting | bytes 8912896 | tf_op jit(solution)/shard_map/reshape | solution.py:56
  436.4 8.6 %reshape.141 = f32[1088,2048]{1,0:T(8,128)} reshape(bf16[64,17,2048]{2,1,0:T(8,128)(2,1)} %all_to_all.31) | data formatting | bytes 13369344 | tf_op jit(solution)/shard_map/convert_element_type | solution.py:69
  445.0 7.0 %fusion.6 = bf16[1088]{0:T(1024)(128)(2,1)S(1)} fusion(f32[1088,2048]{1,0:T(8,128)} %reshape.141, bf16[1088,384]{1,0:T(8,128)(2,1)} %get-tuple-element.20, bf16[1,2048,384]{2,1,0:T(8,128)(2,1)} %param.11), kind=kOutput, calls=%fused_computation.21 | convolution fusion | flops 1715731456 | bytes 11323520 | tf_op jit(solution)/shard_map/dot_general | solution.py:14
  468.4 6.8 %convolution_convert_fusion = bf16[1088,2048]{1,0:T(8,128)(2,1)} fusion(bf16[1,2048,768]{2,1,0:T(8,128)(2,1)S(1)} %copy-done, bf16[1088,384]{1,0:T(8,128)(2,1)} %get-tuple-element.19, bf16[1088,384]{1,0:T(8,128)(2,1)} %get-tuple-element.18), kind=kOutput, calls=%fused_computation.9 | convolution fusion | flops 3428122624 | bytes 9273344 | tf_op jit(solution)/shard_map/dot_general | solution.py:14
  475.2 7.6 %reshape.135 = bf16[64,17,2048]{2,1,0:T(8,128)(2,1)} reshape(bf16[1088,2048]{1,0:T(8,128)(2,1)} %convolution_convert_fusion) | data formatting | bytes 8912896 | tf_op jit(solution)/shard_map/reshape | solution.py:79
  482.8 10.5 %all-to-all-start.3 = ((bf16[64,17,2048]{2,1,0:T(8,128)(2,1)}), bf16[64,17,2048]{2,1,0:T(8,128)(2,1)}, u32[]{:S(2)}, u32[]{:S(2)}) async-start(bf16[64,17,2048]{2,1,0:T(8,128)(2,1)} %reshape.135), calls=%async_computation.3 | async-start | bytes 12582912 | tf_op jit(solution)/shard_map/all_to_all | solution.py:78
  493.5 6.8 %gather_fusion.4 = bf16[1024]{0:T(1024)(128)(2,1)S(1)} fusion(bf16[1088]{0:T(1024)(128)(2,1)S(1)} %reshape.138, s32[1024]{0:T(1024)S(1)} %broadcast_clamp_fusion), kind=kCustom, calls=%fused_computation.4 | custom fusion | bytes 8192 | tf_op jit(solution)/shard_map/gather | solution.py:97
  501.1 133.0 %all-to-all-done.3 = bf16[64,17,2048]{2,1,0:T(8,128)(2,1)} async-done(((bf16[64,17,2048]{2,1,0:T(8,128)(2,1)}), bf16[64,17,2048]{2,1,0:T(8,128)(2,1)}, u32[]{:S(2)}, u32[]{:S(2)}) %all-to-all-start.3) | async-done | bytes 4456480 | tf_op jit(solution)/shard_map/all_to_all | solution.py:78
  634.1 7.8 %reshape.136 = bf16[1088,2048]{1,0:T(8,128)(2,1)} reshape(bf16[64,17,2048]{2,1,0:T(8,128)(2,1)} %all-to-all-done.3) | data formatting | bytes 8912896 | tf_op jit(solution)/shard_map/reshape | solution.py:93
  641.9 11.7 %gather_fusion.3 = bf16[1024,2048]{1,0:T(8,128)(2,1)} fusion(bf16[1088,2048]{1,0:T(8,128)(2,1)} %reshape.136, s32[1024]{0:T(1024)S(1)} %broadcast_clamp_fusion), kind=kCustom, calls=%fused_computation.3 | custom fusion | bytes 8392704 | tf_op jit(solution)/shard_map/gather | solution.py:93
  653.6 5.9 bitcast_reduce_fusion
  (71 shorter events, 49.7 us)
Async XLA Ops:
  7.2 419.0 %copy-start = (bf16[1,2048,768]{2,1,0:T(8,128)(2,1)S(1)}, bf16[1,2048,768]{2,1,0:T(8,128)(2,1)}, u32[]{:S(2)}) copy-start(bf16[1,2048,768]{2,1,0:T(8,128)(2,1)} %param.10) | copy-start | bytes 9437188
  57.9 62.1 %all-to-all-start = ((bf16[64,1,17]{2,1,0:T(2,128)(2,1)}), bf16[64,1,17]{2,1,0:T(2,128)(2,1)S(1)}, u32[]{:S(2)}, u32[]{:S(2)}) async-start(bf16[64,1,17]{2,1,0:T(2,128)(2,1)} %all_to_all.25), calls=%async_computation | async-start | bytes 65536 | tf_op jit(solution)/shard_map/all_to_all | solution.py:54
  271.6 146.8 %all-to-all-start.2 = ((bf16[64,17,2048]{2,1,0:T(8,128)(2,1)}), bf16[64,17,2048]{2,1,0:T(8,128)(2,1)}, u32[]{:S(2)}, u32[]{:S(2)}) async-start(bf16[64,17,2048]{2,1,0:T(8,128)(2,1)} %get-tuple-element.21), calls=%async_computation.2 | async-start | bytes 12582912 | tf_op jit(solution)/shard_map/all_to_all | solution.py:52
  277.5 381.9 %reduce-scatter.2.cloned.1.call-start = ((), (), s32[]{:S(2)}) async-start(), calls=%async_computation.6 | async-start | bytes 5898240 | tf_op jit(solution)/shard_map/reduce_scatter | solution.py:98
  418.4 13.4 %slice-start.2 = ((s8[4456448]{0:T(1024)(128)(4,1)}), s8[262144]{0:T(1024)(128)(4,1)S(1)}, s32[]{:S(2)}) async-start(s8[4456448]{0:T(1024)(128)(4,1)} %bitcast.42), calls=%async_computation.9 | async-start | bytes 524288
  426.2 5.6 slice-start.3
  426.2 5.6 copy-start.3
  436.4 18.2 %slice-start = ((s8[4456448]{0:T(1024)(128)(4,1)}), s8[262144]{0:T(1024)(128)(4,1)S(1)}, s32[]{:S(2)}) async-start(s8[4456448]{0:T(1024)(128)(4,1)} %bitcast.40), calls=%async_computation.7 | async-start | bytes 524288
  445.0 7.0 %copy-start.1 = (f32[1088,2048]{1,0:T(8,128)S(1)}, f32[1088,2048]{1,0:T(8,128)}, u32[]{:S(2)}) copy-start(f32[1088,2048]{1,0:T(8,128)} %reshape.141) | copy-start | bytes 26738692
  445.0 7.0 %copy-start.2 = (bf16[1088,384]{1,0:T(8,128)(2,1)S(1)}, bf16[1088,384]{1,0:T(8,128)(2,1)}, u32[]{:S(2)}) copy-start(bf16[1088,384]{1,0:T(8,128)(2,1)} %get-tuple-element.20) | copy-start | bytes 2506756
  445.0 9.6 %slice-start.1 = ((s8[4456448]{0:T(1024)(128)(4,1)}), s8[4194304]{0:T(1024)(128)(4,1)S(1)}, s32[]{:S(2)}) async-start(s8[4456448]{0:T(1024)(128)(4,1)} %bitcast.40), calls=%async_computation.8 | async-start | bytes 8388608
  452.0 2.6 copy-start.4
  452.1 2.6 copy-start.5
  462.6 20.2 %all-to-all-start.4 = ((bf16[64,1,17]{2,1,0:T(2,128)(2,1)}), bf16[64,1,17]{2,1,0:T(2,128)(2,1)S(1)}, u32[]{:S(2)}, u32[]{:S(2)}) async-start(bf16[64,1,17]{2,1,0:T(2,128)(2,1)} %convert_element_type.85), calls=%async_computation.4 | async-start | bytes 65536 | tf_op jit(solution)/shard_map/all_to_all | solution.py:85
  482.8 151.3 %all-to-all-start.3 = ((bf16[64,17,2048]{2,1,0:T(8,128)(2,1)}), bf16[64,17,2048]{2,1,0:T(8,128)(2,1)}, u32[]{:S(2)}, u32[]{:S(2)}) async-start(bf16[64,17,2048]{2,1,0:T(8,128)(2,1)} %reshape.135), calls=%async_computation.3 | async-start | bytes 12582912 | tf_op jit(solution)/shard_map/all_to_all | solution.py:78
Sparse Core Ops, SparseCore 0:
  462.0 50.1 reduce-scatter.1
where the time goes:
time: 679 us; the launch traced here: 675 us
  waiting for transfers between devices  259 us (38%)
  blocking collectives  152 us (22%)
  local copies, waits for them, and re-layouts  122 us (18%)
  other arithmetic  61.4 us (9%)
  starting transfers between devices  35.4 us (5%)
  matrix products  31.1 us (5%)
  between operations  14.3 us (2%)
    all_to_all x1, blocking collectives, on_device(): lax.all_to_all(send_grads, 'expert', split_axis=0, concat_axis=0, tiled=T...  152 us
    all_to_all x1, waiting for transfers between devices, on_device(): lax.all_to_all(route_grad.reshape(expert_count, capacity, width), 'expert...  133 us
    all_to_all x1, waiting for transfers between devices, on_device(): lax.all_to_all(send_tokens, 'expert', split_axis=0, concat_axis=0, tiled=...  126 us
    another operation x2, other arithmetic  31.1 us
    gather x2, local copies, waits for them, and re-layouts, on_device(): out_grad[token_pick]  19.3 us
    gather x2, local copies, waits for them, and re-layouts, on_device(): tokens[token_pick]  19.3 us
    dot_general x2, matrix products, contract_cols(): lax.dot_general(left, right, (((1,), (1,)), ((), ())), preferred_element_...  13.8 us
  transfers between devices with their start and end apart: 5, of which 2 were waited for; matrix products, arithmetic and copies ran while one was open for 17% of the time, Pallas kernels for 0%

commit v1 on v0

v1 whole, which is shorter than its diff:
```python
import functools

import jax
import jax.numpy as jnp
from jax import lax
from jax.experimental import pallas as pl
from jax.experimental.pallas import tpu as pltpu
from jax.sharding import PartitionSpec as P

MESH = pl.DeviceIdType.MESH
BF = jnp.bfloat16
F32 = jnp.float32

NZ = 8
COL = 8
TOK = 128
D = 2048
FF = 384
SLOT = 16
MAIN = COL * SLOT
ROWS = NZ * MAIN + COL * NZ
BACK = D + 128
OVB = D // 2 + 128
CW = 256


def iota(shape, dim):
    return lax.broadcasted_iota(jnp.int32, shape, dim)


def dot(a, b):
    return jnp.dot(a, b, preferred_element_type=F32)


def dot_nt(a, b):
    return lax.dot_general(a, b, (((1,), (1,)), ((), ())), preferred_element_type=F32)


def dot_tn(a, b):
    return lax.dot_general(a, b, (((0,), (0,)), ((), ())), preferred_element_type=F32)


def tile(n, width=CW):
    return pl.ds(pl.multiple_of(n * width, width), width)


def rows16(start, count):
    return pl.ds(pl.multiple_of(start, 16), count)


def mask(cond, dtype=BF):
    return jnp.where(cond, 1.0, 0.0).astype(dtype)


def kernel(
    tok_ref, dy_ref, ids_ref, probs_ref, wgu_hbm, wdn_hbm,
    out_tok, out_prob, out_gu, out_dn,
    wgu, wdn, meta_own, meta_all, sel, sel_t, sov_t, blk, sendbuf, ovf32, ovsend, ovrecv,
    xs, gu, hg, hbuf, dgu, retbuf, retrecv, retov, retovr, rovf, tf, rsr, gsend, grecv,
    w_sem, meta_s, meta_r, ag_s, ag_r, d_s, d_r, ov_s, ov_r, r_s, r_r, ro_s, ro_r, rs_s, rs_r, g_s, g_r,
):
    e = lax.axis_index("expert")
    x = lax.axis_index("dp")
    y, z, c = e // 16, (e // 2) % 8, e % 2
    s = y * 2 + c
    sgn = 1 - 2 * c
    expert_lane = z * 8 + s

    def zdev(k):
        return ((y * 8 + (z + k + 8) % 8) * 2 + c, x)

    def coldev(t):
        return (((t // 2) * 8 + z) * 2 + t % 2, x)

    def xdev(k):
        return (e, (x + k + 4) % 4)

    def remote(src, dst, ss, rs, dev):
        return pltpu.make_async_remote_copy(
            src_ref=src, dst_ref=dst, send_sem=ss, recv_sem=rs, device_id=dev, device_id_type=MESH
        )

    def loop(lo, hi, fn):
        def step(i, carry):
            fn(i)
            return carry

        lax.fori_loop(lo, hi, step, 0)

    def meta_copy(i):
        return remote(
            meta_own.at[(z + i) % 8], meta_all.at[i], meta_s.at[i], meta_r.at[i], zdev(i)
        )

    def ag_copy(src, pos, p, k):
        return remote(src, blk.at[pos - 1, p], ag_s.at[pos - 1, p], ag_r.at[pos - 1, p], zdev(k))

    def row_copy(pos, p, i):
        t = (s + i) % 8
        return remote(
            sendbuf.at[pos, p, rows16(t * SLOT, SLOT)],
            xs.at[p, rows16(pos * MAIN + s * SLOT, SLOT)],
            d_s.at[pos * 2 + p, i],
            d_r.at[pos * 2 + p, i],
            coldev(t),
        )

    def over_copy(i):
        t = (s + i) % 8
        return remote(
            ovsend.at[rows16(t * 16, 16)], ovrecv.at[rows16(s * 16, 16)], ov_s.at[i], ov_r.at[i], coldev(t)
        )

    def back_copy(pos, i):
        t = (s + i) % 8
        return remote(
            retbuf.at[rows16(pos * MAIN + t * SLOT, SLOT)],
            retrecv.at[pos, rows16(s * SLOT, SLOT)],
            r_s.at[pos, i],
            r_r.at[pos, i],
            coldev(t),
        )

    def back_over_copy(i):
        t = (s + i) % 8
        return remote(
            retov.at[rows16(t * 16, 16)], retovr.at[rows16(s * 16, 16)], ro_s.at[i], ro_r.at[i], coldev(t)
        )

    def sum_copy(pos, piece, k):
        return remote(
            retbuf.at[rows16(pos * MAIN + piece * 64, 64)],
            rsr.at[pos - 1, rows16(piece * 64, 64)],
            rs_s.at[pos - 1, piece],
            rs_r.at[pos - 1, piece],
            zdev(k),
        )

    def grad_copy(slot, k):
        return remote(
            gsend.at[slot % 2], grecv.at[slot], g_s.at[slot], g_r.at[slot], xdev(k)
        )

    barrier = pltpu.get_barrier_semaphore()
    for i in range(1, 8):
        pl.semaphore_signal(barrier, inc=1, device_id=zdev(i), device_id_type=MESH)
        pl.semaphore_signal(barrier, inc=1, device_id=coldev((s + i) % 8), device_id_type=MESH)
    for k in (-1, 1):
        pl.semaphore_signal(barrier, inc=1, device_id=xdev(k), device_id_type=MESH)
    pl.semaphore_wait(barrier, 16)

    for p, ref in ((0, tok_ref), (1, dy_ref)):
        ag_copy(ref, 1, p, sgn).start()
        ag_copy(ref, 2, p, -sgn).start()
    w_gu_copy = pltpu.make_async_copy(wgu_hbm, wgu, w_sem.at[0])
    w_dn_copy = pltpu.make_async_copy(wdn_hbm, wdn, w_sem.at[1])
    w_gu_copy.start()
    w_dn_copy.start()

    def by_z(ids):
        return ((ids // 2) % 8) * 8 + (ids // 16) * 2 + ids % 2

    eye8 = mask(iota((8, 8), 0) == iota((8, 8), 1))
    ids_t = dot_nt(eye8, by_z(ids_ref[...]).astype(F32).astype(BF))
    probs_t = dot_nt(eye8, probs_ref[...])
    lane_of = iota((64, TOK), 0).astype(F32)
    named = jnp.zeros((64, TOK), F32)
    weight = jnp.zeros((64, TOK), F32)
    for k in range(8):
        hit = ids_t[k : k + 1, :] == lane_of
        named += jnp.where(hit, 1.0, 0.0)
        weight += jnp.where(hit, probs_t[k : k + 1, :], 0.0)
    before = mask(iota((TOK, TOK), 0) < iota((TOK, TOK), 1))
    rank = jnp.where(named > 0.0, dot(named.astype(BF), before), -1.0)
    for k in range(NZ):
        meta_own[k, 0:8, :] = rank[k * 8 : k * 8 + 8]
        meta_own[k, 8:16, :] = weight[k * 8 : k * 8 + 8]
    loop(1, 8, lambda i: meta_copy(i).start())

    def build(pos, info):
        ranks, weights = info[0:8], info[8:16]

        def spread(a, n):
            return jnp.concatenate([jnp.broadcast_to(a[k : k + 1], (n, TOK)) for k in range(8)], axis=0)

        hit = spread(ranks, SLOT) == (iota((MAIN, TOK), 0) % SLOT).astype(F32)
        over = ranks == float(SLOT)
        none = jnp.zeros((8, TOK), F32)
        one = jnp.where(hit, 1.0, 0.0)
        sel[0, pos, 0:MAIN, :] = one.astype(BF)
        sel[0, pos, MAIN : MAIN + 16, :] = jnp.concatenate([jnp.where(over, 1.0, 0.0), none], axis=0).astype(BF)
        sel[1, pos, 0:MAIN, :] = jnp.where(hit, spread(weights, SLOT), 0.0).astype(BF)
        sel[1, pos, MAIN : MAIN + 16, :] = jnp.concatenate([jnp.where(over, weights, 0.0), none], axis=0).astype(BF)
        sel_t[pos] = one.T.astype(BF)
        mine = (spread(ranks, 8) == float(SLOT)) & (iota((64, TOK), 0) % 8 == pos)
        wide = jnp.concatenate([jnp.where(mine, 1.0, 0.0), jnp.zeros((64, TOK), F32)], axis=0)
        sov_t[pos] = wide.T.astype(BF)

    def pick(pos, p, ref):
        def column(n):
            got = dot(sel[p, pos], ref[:, tile(n)])
            sendbuf[pos, p, :, tile(n)] = got[:MAIN].astype(BF)
            ovf32[p, pl.ds(pl.multiple_of(pos * 8, 8), 8), tile(n)] = got[MAIN : MAIN + 8]

        loop(0, D // CW, column)
        loop(1, 8, lambda i: row_copy(pos, p, i).start())
        xs[p, rows16(pos * MAIN + s * SLOT, SLOT), :] = sendbuf[pos, p, rows16(s * SLOT, SLOT), :]

    def await_rows(pos):
        loop(1, 8, lambda i: row_copy(pos, 0, i).wait_recv())
        loop(1, 8, lambda i: row_copy(pos, 1, i).wait_recv())

    def expert(row0, count):
        rows = rows16(row0, count)

        def first(n):
            gu[0:count, tile(n)] = dot(xs[0, rows, :], wgu[:, tile(n)])

        loop(0, 2 * FF // CW, first)

        def second(n):
            hg[0:count, tile(n, 128)] = dot(xs[1, rows, :], wdn[:, tile(n, 128)])

        loop(0, FF // 128, second)

        def middle(n):
            part, whole = rows16(n * 32, 32), rows16(row0 + n * 32, 32)
            gate, up, grad = gu[part, 0:FF], gu[part, FF : 2 * FF], hg[part, :]
            sig = jax.nn.sigmoid(gate)
            silu = gate * sig
            act = (silu * up).astype(BF)
            hbuf[whole, :] = act
            dgu[whole, 0:FF] = (grad * up * sig * (1.0 + gate * (1.0 - sig))).astype(BF)
            dgu[whole, FF : 2 * FF] = (grad * silu).astype(BF)
            router = jnp.sum(grad * act.astype(F32), axis=1, keepdims=True)
            retbuf[whole, D:BACK] = jnp.where(iota((32, 128), 1) == expert_lane, router, 0.0).astype(BF)

        loop(0, count // 32, middle)

        def last(n):
            retbuf[rows, tile(n)] = dot_nt(dgu[rows, :], wgu[tile(n), :]).astype(BF)

        loop(0, D // CW, last)

    build(0, meta_own[z])
    pick(0, 0, tok_ref)
    pick(0, 1, dy_ref)
    w_gu_copy.wait()
    w_dn_copy.wait()

    r128, c64 = iota((128, 64), 0), iota((128, 64), 1)
    r64, c128 = iota((64, 128), 0), iota((64, 128), 1)

    def turn(d):
        odd, even = 2 * d - 1, 2 * d
        up_at, down_at = (8 + sgn * d) % 8, (8 - sgn * d) % 8
        meta_copy(up_at).wait_recv()
        build(odd, meta_all[up_at])

        @pl.when(d < 4)
        def _():
            meta_copy(down_at).wait_recv()
            build(even, meta_all[down_at])

        def piece(p):
            ag_copy(tok_ref, odd, p, sgn).wait_recv()

            @pl.when(d < 4)
            def _():
                ag_copy(blk.at[odd - 1, p], odd + 2, p, sgn).start()

            pick(odd, p, blk.at[odd - 1, p])

            @pl.when(d < 4)
            def _():
                ag_copy(tok_ref, even, p, -sgn).wait_recv()

                @pl.when(d < 3)
                def _():
                    ag_copy(blk.at[even - 1, p], even + 2, p, -sgn).start()

                pick(even, p, blk.at[even - 1, p])

        loop(0, 2, piece)

        @pl.when(d == 4)
        def _():
            where_of = c64 == (r128 % 8) * 8 + r128 // 16
            first, second = mask((r128 % 16 < 8) & where_of), mask((r128 % 16 >= 8) & where_of)

            def column(n):
                a, b = ovf32[0, :, tile(n)].astype(BF), ovf32[1, :, tile(n)].astype(BF)
                ovsend[:, tile(n)] = (dot(first, a) + dot(second, b)).astype(BF)

            loop(0, D // CW, column)
            loop(1, 8, lambda i: over_copy(i).start())
            ovrecv[rows16(s * 16, 16), :] = ovsend[rows16(s * 16, 16), :]

        @pl.when(d >= 2)
        def _():
            await_rows(2 * d - 4)
            await_rows(2 * d - 3)
            expert((2 * d - 4) * MAIN, 2 * MAIN)

    loop(1, 5, turn)

    await_rows(6)
    await_rows(7)
    loop(1, 8, lambda i: over_copy(i).wait_recv())
    take_lo = mask(c128 == (r64 // 8) * 16 + r64 % 8)
    take_hi = mask(c128 == (r64 // 8) * 16 + 8 + r64 % 8)

    def unpack(n):
        got = ovrecv[:, tile(n)]
        xs[0, NZ * MAIN : ROWS, tile(n)] = dot(take_lo, got).astype(BF)
        xs[1, NZ * MAIN : ROWS, tile(n)] = dot(take_hi, got).astype(BF)

    loop(0, D // CW, unpack)
    expert(6 * MAIN, ROWS - 6 * MAIN)

    put_lo = mask((r128 % 16 < 8) & (c64 == (r128 // 16) * 8 + r128 % 16))
    put_hi = mask((r128 % 16 >= 8) & (c64 == (r128 // 16) * 8 + r128 % 16 - 8))
    over_rows = pl.ds(NZ * MAIN, COL * NZ)

    def pack(n):
        lo, hi = retbuf[over_rows, tile(n)], retbuf[over_rows, tile(n + 4)]
        retov[:, tile(n)] = (dot(put_lo, lo) + dot(put_hi, hi)).astype(BF)

    loop(0, D // 2 // CW, pack)
    retov[:, D // 2 : OVB] = dot(put_lo, retbuf[over_rows, D:BACK]).astype(BF)
    loop(1, 8, lambda i: back_over_copy(i).start())
    retovr[rows16(s * 16, 16), :] = retov[rows16(s * 16, 16), :]

    def send_back(k):
        pos = NZ - 1 - k
        loop(1, 8, lambda i: back_copy(pos, i).start())
        retrecv[pos, rows16(s * SLOT, SLOT), :] = retbuf[rows16(pos * MAIN + s * SLOT, SLOT), :]

    loop(0, NZ, send_back)

    def weight_grad(j, emit):
        def half(m):
            cols = pl.ds(pl.multiple_of(j * 512 + m * CW, CW), CW)
            emit(m, dot_tn(xs[0, :, cols], dgu[...]), dot_tn(xs[1, :, cols], hbuf[...]))

        loop(0, 2, half)

    def emit_send(slot):
        def emit(m, a, b):
            gsend[slot, tile(m), 0 : 2 * FF] = a.astype(BF)
            gsend[slot, tile(m), 2 * FF :] = b.astype(BF)

        return emit

    weight_grad((x + 2) % 4, emit_send(0))
    grad_copy(0, sgn).start()
    weight_grad((x - sgn + 4) % 4, emit_send(1))
    grad_copy(1, -sgn).start()

    def emit_own(m, a, b):
        out_gu[tile(m), :] = a
        out_dn[tile(m), :] = b

    weight_grad(x, emit_own)

    loop(1, 8, lambda i: back_over_copy(i).wait_recv())

    def unpack_back(n):
        got = retovr[:, tile(n)]
        rovf[0:64, tile(n)] = dot(take_lo, got).astype(BF)
        rovf[0:64, tile(n + 4)] = dot(take_hi, got).astype(BF)

    loop(0, D // 2 // CW, unpack_back)
    rovf[0:64, D:BACK] = dot(take_lo, retovr[:, D // 2 : OVB]).astype(BF)
    rovf[64:128, :] = jnp.zeros((64, BACK), BF)

    def combine(pos):
        loop(1, 8, lambda i: back_copy(pos, i).wait_recv())

        def column(n):
            tf[:, tile(n)] = dot(sel_t[pos], retrecv[pos, :, tile(n)]) + dot(sov_t[pos], rovf[:, tile(n)])

        loop(0, D // CW, column)
        tf[:, D:BACK] = dot(sel_t[pos], retrecv[pos, :, D:BACK]) + dot(sov_t[pos], rovf[:, D:BACK])

    def pass_on(pos, k, has_more):
        combine(pos)
        loop(1, 8, lambda i: back_copy(pos, i).wait_send())

        def piece(h):
            @pl.when(has_more)
            def _():
                sum_copy(pos + 2, h, k).wait_recv()

                def part(n):
                    at = rows16(h * 64 + n * 16, 16)
                    total = tf[at, :] + rsr[pos + 1, at, :].astype(F32)
                    retbuf[rows16(pos * MAIN + h * 64 + n * 16, 16), :] = total.astype(BF)

                loop(0, 4, part)

            @pl.when(jnp.logical_not(has_more))
            def _():
                def part(n):
                    at = rows16(h * 64 + n * 16, 16)
                    retbuf[rows16(pos * MAIN + h * 64 + n * 16, 16), :] = tf[at, :].astype(BF)

                loop(0, 4, part)

            sum_copy(pos, h, k).start()

        loop(0, 2, piece)

    def back_turn(k):
        d = 4 - k
        pass_on(2 * d - 1, -sgn, d < 4)

        @pl.when(d < 4)
        def _():
            pass_on(2 * d, sgn, d < 3)

        @pl.when(d == 2)
        def _():
            grad_copy(0, sgn).wait()

            def emit(m, a, b):
                got = grecv[0, tile(m), :].astype(F32)
                gsend[0, tile(m), 0 : 2 * FF] = (a + got[:, 0 : 2 * FF]).astype(BF)
                gsend[0, tile(m), 2 * FF :] = (b + got[:, 2 * FF :]).astype(BF)

            weight_grad((x + sgn + 4) % 4, emit)
            grad_copy(2, sgn).start()

    loop(0, 4, back_turn)

    combine(0)
    for pos in (1, 2):
        for h in (0, 1):
            sum_copy(pos, h, sgn).wait_recv()

    def finish(n):
        at = rows16(n * 16, 16)
        total = tf[at, :] + rsr[0, at, :].astype(F32) + rsr[1, at, :].astype(F32)
        out_tok[at, :] = total[:, 0:D].astype(BF)
        tf[at, D:BACK] = total[:, D:BACK]

    loop(0, TOK // 16, finish)
    router = tf[:, D:BACK]
    ids = by_z(ids_ref[...])
    found = jnp.zeros((TOK, 8), F32)
    for k in range(8):
        hit = ids[:, k : k + 1] == iota((TOK, 128), 1)
        value = jnp.sum(jnp.where(hit, router, 0.0), axis=1, keepdims=True)
        found = jnp.where(iota((TOK, 8), 1) == k, value, found)
    out_prob[...] = (found / probs_ref[...].astype(F32)).astype(BF)

    grad_copy(1, -sgn).wait()
    grad_copy(2, sgn).wait()

    def add_grads(n):
        at = rows16(n * 32, 32)
        more = grecv[1, at, :].astype(F32) + grecv[2, at, :].astype(F32)
        out_gu[at, :] = out_gu[at, :] + more[:, 0 : 2 * FF]
        out_dn[at, :] = out_dn[at, :] + more[:, 2 * FF :]

    loop(0, 512 // 32, add_grads)

    loop(1, 8, lambda i: meta_copy(i).wait_send())
    loop(1, 8, lambda i: over_copy(i).wait_send())
    loop(1, 8, lambda i: back_over_copy(i).wait_send())
    loop(1, 8, lambda i: back_copy(0, i).wait_send())

    def drain(pos):
        loop(1, 8, lambda i: row_copy(pos, 0, i).wait_send())
        loop(1, 8, lambda i: row_copy(pos, 1, i).wait_send())

    loop(0, NZ, drain)

    def drain_ring(pos):
        def piece(h):
            ag_copy(tok_ref, pos, h, sgn).wait_send()
            sum_copy(pos, h, sgn).wait_send()

        loop(0, 2, piece)

    loop(1, 8, drain_ring)


def on_device(tokens, out_grad, expert_ids, route_probs, w_gate_up, w_down):
    vm, dma = pltpu.VMEM, pltpu.SemaphoreType.DMA
    inside = pl.BlockSpec(memory_space=pltpu.VMEM)
    token_grad, prob_grad, grad_gu, grad_dn = pl.pallas_call(
        kernel,
        out_shape=(
            jax.ShapeDtypeStruct((TOK, D), BF),
            jax.ShapeDtypeStruct((TOK, 8), BF),
            jax.ShapeDtypeStruct((512, 2 * FF), F32),
            jax.ShapeDtypeStruct((512, FF), F32),
        ),
        in_specs=[inside] * 4 + [pl.BlockSpec(memory_space=pl.ANY)] * 2,
        out_specs=(inside,) * 4,
        scratch_shapes=[
            vm((D, 2 * FF), BF),
            vm((D, FF), BF),
            vm((NZ, 16, TOK), F32),
            vm((NZ, 16, TOK), F32),
            vm((2, NZ, MAIN + 16, TOK), BF),
            vm((NZ, TOK, MAIN), BF),
            vm((NZ, TOK, 128), BF),
            vm((NZ - 1, 2, TOK, D), BF),
            vm((NZ, 2, MAIN, D), BF),
            vm((2, 64, D), F32),
            vm((128, D), BF),
            vm((128, D), BF),
            vm((2, ROWS, D), BF),
            vm((320, 2 * FF), F32),
            vm((320, FF), F32),
            vm((ROWS, FF), BF),
            vm((ROWS, 2 * FF), BF),
            vm((ROWS, BACK), BF),
            vm((NZ, MAIN, BACK), BF),
            vm((128, OVB), BF),
            vm((128, OVB), BF),
            vm((128, BACK), BF),
            vm((TOK, BACK), F32),
            vm((NZ - 1, TOK, BACK), BF),
            vm((2, 512, 3 * FF), BF),
            vm((3, 512, 3 * FF), BF),
            dma((2,)),
            dma((8,)), dma((8,)),
            dma((7, 2)), dma((7, 2)),
            dma((16, 8)), dma((16, 8)),
            dma((8,)), dma((8,)),
            dma((8, 8)), dma((8, 8)),
            dma((8,)), dma((8,)),
            dma((7, 2)), dma((7, 2)),
            dma((3,)), dma((3,)),
        ],
        compiler_params=pltpu.CompilerParams(
            collective_id=0, has_side_effects=True, vmem_limit_bytes=62 * 2**20
        ),
        cost_estimate=pl.CostEstimate(flops=15 * 10**9, bytes_accessed=10**7, transcendentals=10**6),
        name="routed_backward",
    )(tokens, out_grad, expert_ids, route_probs, w_gate_up[0], w_down[0])
    return token_grad, prob_grad, grad_gu[None], grad_dn[None]


def solution(mesh):
    in_specs = (
        P(("expert", "dp"), None),
        P(("expert", "dp"), None),
        P(("expert", "dp"), None),
        P(("expert", "dp"), None),
        P("expert", None, None),
        P("expert", None, None),
    )
    out_specs = (
        P(("expert", "dp"), None),
        P(("expert", "dp"), None),
        P("expert", "dp", None),
        P("expert", "dp", None),
    )
    return jax.shard_map(
        on_device, mesh=mesh, in_specs=in_specs, out_specs=out_specs, check_vma=False
    )
```

time: 679 us -> 215 us (0.32)
  waiting for transfers between devices: 259 us -> 0 us
  Pallas kernels: 0 us -> 204 us
  blocking collectives: 152 us -> 0 us
  local copies, waits for them, and re-layouts: 122 us -> 9.71 us
  other arithmetic: 61.4 us -> 0 us
  starting transfers between devices: 35.4 us -> 0 us
  matrix products: 31.1 us -> 0 us
  between operations: 14.3 us -> 0.64 us
    all_to_all x4 -> x0, waiting for transfers between devices: 259 us -> none  [the longest x1 133 us: on_device(): lax.all_to_all(route_grad.reshape(expert_count, capacity, width), 'expert...]
    pallas_call x0 -> x1, Pallas kernels: none -> 204 us  [on_device(): pl.pallas_call(kernel, out_shape=(jax.ShapeDtypeStruct((TOK, D), BF), jax...]
    all_to_all x1 -> x0, blocking collectives: 152 us -> none  [on_device(): lax.all_to_all(send_grads, 'expert', split_axis=0, concat_axis=0, tiled=T...]
    gather x7 -> x0, local copies, waits for them, and re-layouts: 63.9 us -> none  [the longest x2 19.3 us: on_device(): out_grad[token_pick]]
    all_to_all x4 -> x0, starting transfers between devices: 35.4 us -> none  [the longest x1 13.2 us: on_device(): lax.all_to_all(send_probs, 'expert', split_axis=0, concat_axis=0, tiled=T...]
    dot_general x6 -> x0, matrix products: 31.1 us -> none  [the longest x2 13.8 us: contract_cols(): lax.dot_general(left, right, (((1,), (1,)), ((), ())), preferred_element_...]
    another operation x2 -> x0, other arithmetic: 31.1 us -> none
    reshape x6 -> x0, local copies, waits for them, and re-layouts: 23.5 us -> none  [the longest x1 7.79 us: on_device(): x_in = recv_tokens.reshape(slot_total, width)]
  transfers between devices with their start and end apart: 5 -> 0, of which waited for: 2 -> 0; matrix products, arithmetic and copies ran while one was open for 17% -> 0% of each run, Pallas kernels for 0% -> 0%
where the time goes in v1:
time: 215 us; the launch traced here: 214 us
  Pallas kernels  204 us (95%)
  local copies, waits for them, and re-layouts  9.71 us (5%)
    pallas_call x1, Pallas kernels, on_device(): pl.pallas_call(kernel, out_shape=(jax.ShapeDtypeStruct((TOK, D), BF), jax...  204 us
    unnamed x8, local copies, waits for them, and re-layouts  9.71 us

profile of v1, /device:TPU:1, one launch (start us, length us, event | category | flops | bytes accessed | tf_op | source)
XLA Modules:
  0.0 214.0 jit_solution(16164002256738727767)
XLA Ops:
  0.6 1.4 copy.11.probs_ref
  2.0 1.4 copy.10.ids_ref
  3.4 203.7 %routed_backward.1 = (bf16[128,2048]{1,0:T(8,128)(2,1)}, bf16[128,8]{1,0:T(8,128)(2,1)}, f32[512,768]{1,0:T(8,128)}, f32[512,384]{1,0:T(8,128)}) custom-call(bf16[128,2048]{1,0:T(8,128)(2,1)} %tok_ref.1, bf16[128,2048]{1,0:T(8,128)(2,1)} %dy_ref.1, s32[128,8]{1,0:T(8,128)} %copy.10.ids_ref, bf16[128,8]{1,0:T(8,128)(2,1)} %copy.11.probs_ref, ...), custom_call_target="tpu_custom_call" | custom-call | flops 15000000512 | bytes 10000000 | tf_op jit(solution)/shard_map/routed_backward/pallas_call | solution.py:492
  207.1 1.4 copy.12
  208.6 1.9 copy.16
  210.4 0.0 copy-start
  210.4 2.7 %copy.17 = f32[1,512,768]{2,1,0:T(8,128)} copy(f32[1,512,768]{2,1,0:T(8,128)} %bitcast.4) | data formatting | bytes 3145728
  213.2 0.0 copy-done
  213.2 0.9 copy.18
Async XLA Ops:
  210.4 2.7 %copy-start = (f32[512,384]{1,0:T(8,128)S(1)}, f32[512,384]{1,0:T(8,128)}, u32[]{:S(2)}) copy-start(f32[512,384]{1,0:T(8,128)} %get-tuple-element.11) | copy-start | bytes 2359300

commit v2 on v1

--- a/solution.py
+++ b/solution.py
@@ -21,6 +21,7 @@
 ROWS = NZ * MAIN + COL * NZ
 BACK = D + 128
 OVB = D // 2 + 128
+OVER = (NZ - 1) * MAIN
 CW = 256
 
 
@@ -55,9 +56,9 @@
 def kernel(
     tok_ref, dy_ref, ids_ref, probs_ref, wgu_hbm, wdn_hbm,
     out_tok, out_prob, out_gu, out_dn,
-    wgu, wdn, meta_own, meta_all, sel, sel_t, sov_t, blk, sendbuf, ovf32, ovsend, ovrecv,
+    wgu, wdn, meta_own, meta_all, far, far_in, sel, sel_t, sov_t, blk, sendbuf, ovf32, ovsend, ovrecv,
     xs, gu, hg, hbuf, dgu, retbuf, retrecv, retov, retovr, rovf, tf, rsr, gsend, grecv,
-    w_sem, meta_s, meta_r, ag_s, ag_r, d_s, d_r, ov_s, ov_r, r_s, r_r, ro_s, ro_r, rs_s, rs_r, g_s, g_r,
+    w_sem, far_sem, meta_s, meta_r, ag_s, ag_r, d_s, d_r, ov_s, ov_r, r_s, r_r, ro_s, ro_r, rs_s, rs_r, g_s, g_r,
 ):
     e = lax.axis_index("expert")
     x = lax.axis_index("dp")
@@ -80,6 +81,9 @@
             src_ref=src, dst_ref=dst, send_sem=ss, recv_sem=rs, device_id=dev, device_id_type=MESH
         )
 
+    def base(pos):
+        return pos * MAIN + (pos // (NZ - 1)) * COL * NZ
+
     def loop(lo, hi, fn):
         def step(i, carry):
             fn(i)
@@ -99,7 +103,7 @@
         t = (s + i) % 8
         return remote(
             sendbuf.at[pos, p, rows16(t * SLOT, SLOT)],
-            xs.at[p, rows16(pos * MAIN + s * SLOT, SLOT)],
+            xs.at[p, rows16(base(pos) + s * SLOT, SLOT)],
             d_s.at[pos * 2 + p, i],
             d_r.at[pos * 2 + p, i],
             coldev(t),
@@ -114,7 +118,7 @@
     def back_copy(pos, i):
         t = (s + i) % 8
         return remote(
-            retbuf.at[rows16(pos * MAIN + t * SLOT, SLOT)],
+            retbuf.at[rows16(base(pos) + t * SLOT, SLOT)],
             retrecv.at[pos, rows16(s * SLOT, SLOT)],
             r_s.at[pos, i],
             r_r.at[pos, i],
@@ -129,17 +133,29 @@
 
     def sum_copy(pos, piece, k):
         return remote(
-            retbuf.at[rows16(pos * MAIN + piece * 64, 64)],
+            retbuf.at[rows16(base(pos) + piece * 64, 64)],
             rsr.at[pos - 1, rows16(piece * 64, 64)],
             rs_s.at[pos - 1, piece],
             rs_r.at[pos - 1, piece],
             zdev(k),
         )
 
-    def grad_copy(slot, k):
+    def grad_copy(slot, half, k):
         return remote(
-            gsend.at[slot % 2], grecv.at[slot], g_s.at[slot], g_r.at[slot], xdev(k)
-        )
+            gsend.at[slot % 2, tile(half)],
+            grecv.at[slot, tile(half)],
+            g_s.at[slot, half],
+            g_r.at[slot, half],
+            xdev(k),
+        )
+
+    def far_copy():
+        return remote(far, far_in, far_sem.at[0], far_sem.at[1], zdev(4))
+
+    w_gu_copy = pltpu.make_async_copy(wgu_hbm, wgu, w_sem.at[0])
+    w_dn_copy = pltpu.make_async_copy(wdn_hbm, wdn, w_sem.at[1])
+    w_gu_copy.start()
+    w_dn_copy.start()
 
     barrier = pltpu.get_barrier_semaphore()
     for i in range(1, 8):
@@ -147,23 +163,12 @@
         pl.semaphore_signal(barrier, inc=1, device_id=coldev((s + i) % 8), device_id_type=MESH)
     for k in (-1, 1):
         pl.semaphore_signal(barrier, inc=1, device_id=xdev(k), device_id_type=MESH)
-    pl.semaphore_wait(barrier, 16)
-
-    for p, ref in ((0, tok_ref), (1, dy_ref)):
-        ag_copy(ref, 1, p, sgn).start()
-        ag_copy(ref, 2, p, -sgn).start()
-    w_gu_copy = pltpu.make_async_copy(wgu_hbm, wgu, w_sem.at[0])
-    w_dn_copy = pltpu.make_async_copy(wdn_hbm, wdn, w_sem.at[1])
-    w_gu_copy.start()
-    w_dn_copy.start()
-
     def by_z(ids):
         return ((ids // 2) % 8) * 8 + (ids // 16) * 2 + ids % 2
 
-    eye8 = mask(iota((8, 8), 0) == iota((8, 8), 1))
-    ids_t = dot_nt(eye8, by_z(ids_ref[...]).astype(F32).astype(BF))
-    probs_t = dot_nt(eye8, probs_ref[...])
-    lane_of = iota((64, TOK), 0).astype(F32)
+    ids_t = by_z(ids_ref[...])
+    probs_t = probs_ref[...].astype(F32)
+    lane_of = iota((64, TOK), 0)
     named = jnp.zeros((64, TOK), F32)
     weight = jnp.zeros((64, TOK), F32)
     for k in range(8):
@@ -175,7 +180,6 @@
     for k in range(NZ):
         meta_own[k, 0:8, :] = rank[k * 8 : k * 8 + 8]
         meta_own[k, 8:16, :] = weight[k * 8 : k * 8 + 8]
-    loop(1, 8, lambda i: meta_copy(i).start())
 
     def build(pos, info):
         ranks, weights = info[0:8], info[8:16]
@@ -203,8 +207,10 @@
             ovf32[p, pl.ds(pl.multiple_of(pos * 8, 8), 8), tile(n)] = got[MAIN : MAIN + 8]
 
         loop(0, D // CW, column)
+
+    def send(pos, p):
         loop(1, 8, lambda i: row_copy(pos, p, i).start())
-        xs[p, rows16(pos * MAIN + s * SLOT, SLOT), :] = sendbuf[pos, p, rows16(s * SLOT, SLOT), :]
+        xs[p, rows16(base(pos) + s * SLOT, SLOT), :] = sendbuf[pos, p, rows16(s * SLOT, SLOT), :]
 
     def await_rows(pos):
         loop(1, 8, lambda i: row_copy(pos, 0, i).wait_recv())
@@ -245,6 +251,26 @@
     build(0, meta_own[z])
     pick(0, 0, tok_ref)
     pick(0, 1, dy_ref)
+    opposite = meta_own[(z + 4) % 8]
+    nobody = jnp.zeros((8, TOK), F32)
+    far_one = jnp.concatenate([jnp.where(opposite[0:8] == float(SLOT), 1.0, 0.0), nobody], axis=0).astype(BF)
+    far_weight = jnp.concatenate([nobody, jnp.where(opposite[0:8] == float(SLOT), opposite[8:16], 0.0)], axis=0).astype(BF)
+
+    def far_rows(n):
+        far[:, tile(n)] = (dot(far_one, tok_ref[:, tile(n)]) + dot(far_weight, dy_ref[:, tile(n)])).astype(BF)
+
+    loop(0, D // CW, far_rows)
+
+    pl.semaphore_wait(barrier, 16)
+
+    ag_copy(tok_ref, 1, 0, sgn).start()
+    ag_copy(tok_ref, 2, 0, -sgn).start()
+    send(0, 0)
+    loop(1, 8, lambda i: meta_copy(i).start())
+    ag_copy(dy_ref, 1, 1, sgn).start()
+    ag_copy(dy_ref, 2, 1, -sgn).start()
+    send(0, 1)
+    far_copy().start()
     w_gu_copy.wait()
     w_dn_copy.wait()
 
@@ -270,6 +296,7 @@
                 ag_copy(blk.at[odd - 1, p], odd + 2, p, sgn).start()
 
             pick(odd, p, blk.at[odd - 1, p])
+            send(odd, p)
 
             @pl.when(d < 4)
             def _():
@@ -280,11 +307,15 @@
                     ag_copy(blk.at[even - 1, p], even + 2, p, -sgn).start()
 
                 pick(even, p, blk.at[even - 1, p])
+                send(even, p)
 
         loop(0, 2, piece)
 
-        @pl.when(d == 4)
+        @pl.when(d == 3)
         def _():
+            far_copy().wait_recv()
+            ovf32[0, 56:64, :] = far_in[...].astype(F32)[0:8]
+            ovf32[1, 56:64, :] = far_in[...].astype(F32)[8:16]
             where_of = c64 == (r128 % 8) * 8 + r128 // 16
             first, second = mask((r128 % 16 < 8) & where_of), mask((r128 % 16 >= 8) & where_of)
 
@@ -305,22 +336,21 @@
     loop(1, 5, turn)
 
     await_rows(6)
-    await_rows(7)
     loop(1, 8, lambda i: over_copy(i).wait_recv())
     take_lo = mask(c128 == (r64 // 8) * 16 + r64 % 8)
     take_hi = mask(c128 == (r64 // 8) * 16 + 8 + r64 % 8)
 
     def unpack(n):
         got = ovrecv[:, tile(n)]
-        xs[0, NZ * MAIN : ROWS, tile(n)] = dot(take_lo, got).astype(BF)
-        xs[1, NZ * MAIN : ROWS, tile(n)] = dot(take_hi, got).astype(BF)
+        xs[0, OVER : OVER + COL * NZ, tile(n)] = dot(take_lo, got).astype(BF)
+        xs[1, OVER : OVER + COL * NZ, tile(n)] = dot(take_hi, got).astype(BF)
 
     loop(0, D // CW, unpack)
-    expert(6 * MAIN, ROWS - 6 * MAIN)
+    expert(6 * MAIN, MAIN + COL * NZ)
 
     put_lo = mask((r128 % 16 < 8) & (c64 == (r128 // 16) * 8 + r128 % 16))
     put_hi = mask((r128 % 16 >= 8) & (c64 == (r128 // 16) * 8 + r128 % 16 - 8))
-    over_rows = pl.ds(NZ * MAIN, COL * NZ)
+    over_rows = pl.ds(OVER, COL * NZ)
 
     def pack(n):
         lo, hi = retbuf[over_rows, tile(n)], retbuf[over_rows, tile(n + 4)]
@@ -331,37 +361,50 @@
     loop(1, 8, lambda i: back_over_copy(i).start())
     retovr[rows16(s * 16, 16), :] = retov[rows16(s * 16, 16), :]
 
-    def send_back(k):
-        pos = NZ - 1 - k
+    def send_back(pos):
         loop(1, 8, lambda i: back_copy(pos, i).start())
-        retrecv[pos, rows16(s * SLOT, SLOT), :] = retbuf[rows16(pos * MAIN + s * SLOT, SLOT), :]
-
-    loop(0, NZ, send_back)
-
-    def weight_grad(j, emit):
-        def half(m):
-            cols = pl.ds(pl.multiple_of(j * 512 + m * CW, CW), CW)
-            emit(m, dot_tn(xs[0, :, cols], dgu[...]), dot_tn(xs[1, :, cols], hbuf[...]))
-
-        loop(0, 2, half)
-
-    def emit_send(slot):
-        def emit(m, a, b):
-            gsend[slot, tile(m), 0 : 2 * FF] = a.astype(BF)
-            gsend[slot, tile(m), 2 * FF :] = b.astype(BF)
-
-        return emit
-
-    weight_grad((x + 2) % 4, emit_send(0))
-    grad_copy(0, sgn).start()
-    weight_grad((x - sgn + 4) % 4, emit_send(1))
-    grad_copy(1, -sgn).start()
-
-    def emit_own(m, a, b):
-        out_gu[tile(m), :] = a
-        out_dn[tile(m), :] = b
-
-    weight_grad(x, emit_own)
+        retrecv[pos, rows16(s * SLOT, SLOT), :] = retbuf[rows16(base(pos) + s * SLOT, SLOT), :]
+
+    send_back(6)
+    await_rows(7)
+    expert(base(7), MAIN)
+    send_back(7)
+
+    def send_pair(k):
+        send_back(4 - 2 * k)
+        send_back(5 - 2 * k)
+
+    loop(0, 2, send_pair)
+    send_back(1)
+    send_back(0)
+
+    def weight_grad(j, m, emit):
+        cols = pl.ds(pl.multiple_of(j * 512 + m * CW, CW), CW)
+        emit(dot_tn(xs[0, :, cols], dgu[...]), dot_tn(xs[1, :, cols], hbuf[...]))
+
+    def first_grads(m):
+        def emit_to(slot):
+            def emit(a, b):
+                gsend[slot, tile(m), 0 : 2 * FF] = a.astype(BF)
+                gsend[slot, tile(m), 2 * FF :] = b.astype(BF)
+
+            return emit
+
+        weight_grad((x + 2) % 4, m, emit_to(0))
+        grad_copy(0, m, sgn).start()
+        weight_grad((x - sgn + 4) % 4, m, emit_to(1))
+        grad_copy(1, m, -sgn).start()
+
+    loop(0, 2, first_grads)
+
+    def own_grads(m):
+        def emit(a, b):
+            out_gu[tile(m), :] = a
+            out_dn[tile(m), :] = b
+
+        weight_grad(x, m, emit)
+
+    loop(0, 2, own_grads)
 
     loop(1, 8, lambda i: back_over_copy(i).wait_recv())
 
@@ -395,7 +438,7 @@
                 def part(n):
                     at = rows16(h * 64 + n * 16, 16)
                     total = tf[at, :] + rsr[pos + 1, at, :].astype(F32)
-                    retbuf[rows16(pos * MAIN + h * 64 + n * 16, 16), :] = total.astype(BF)
+                    retbuf[rows16(base(pos) + h * 64 + n * 16, 16), :] = total.astype(BF)
 
                 loop(0, 4, part)
 
@@ -403,7 +446,7 @@
             def _():
                 def part(n):
                     at = rows16(h * 64 + n * 16, 16)
-                    retbuf[rows16(pos * MAIN + h * 64 + n * 16, 16), :] = tf[at, :].astype(BF)
+                    retbuf[rows16(base(pos) + h * 64 + n * 16, 16), :] = tf[at, :].astype(BF)
 
                 loop(0, 4, part)
 
@@ -411,25 +454,47 @@
 
         loop(0, 2, piece)
 
+    def drain():
+        far_copy().wait_send()
+        loop(1, 8, lambda i: meta_copy(i).wait_send())
+        loop(1, 8, lambda i: over_copy(i).wait_send())
+        loop(1, 8, lambda i: back_over_copy(i).wait_send())
+
+        def drain_rows(pos):
+            loop(1, 8, lambda i: row_copy(pos, 0, i).wait_send())
+            loop(1, 8, lambda i: row_copy(pos, 1, i).wait_send())
+
+        loop(0, NZ, drain_rows)
+
+        def drain_ring(pos):
+            ag_copy(tok_ref, pos, 0, sgn).wait_send()
+            ag_copy(tok_ref, pos, 1, sgn).wait_send()
+
+        loop(1, 8, drain_ring)
+
     def back_turn(k):
-        d = 4 - k
-        pass_on(2 * d - 1, -sgn, d < 4)
-
-        @pl.when(d < 4)
+        @pl.when(k < 3)
         def _():
-            pass_on(2 * d, sgn, d < 3)
-
-        @pl.when(d == 2)
+            pass_on(6 - 2 * k, sgn, k > 0)
+
+        pass_on(7 - 2 * k, -sgn, k > 0)
+
+        @pl.when(k == 0)
         def _():
-            grad_copy(0, sgn).wait()
-
-            def emit(m, a, b):
+            drain()
+
+        @pl.when((k == 1) | (k == 2))
+        def _():
+            m = k - 1
+            grad_copy(0, m, sgn).wait()
+
+            def emit(a, b):
                 got = grecv[0, tile(m), :].astype(F32)
                 gsend[0, tile(m), 0 : 2 * FF] = (a + got[:, 0 : 2 * FF]).astype(BF)
                 gsend[0, tile(m), 2 * FF :] = (b + got[:, 2 * FF :]).astype(BF)
 
-            weight_grad((x + sgn + 4) % 4, emit)
-            grad_copy(2, sgn).start()
+            weight_grad((x + sgn + 4) % 4, m, emit)
+            grad_copy(2, m, sgn).start()
 
     loop(0, 4, back_turn)
 
@@ -446,16 +511,16 @@
 
     loop(0, TOK // 16, finish)
     router = tf[:, D:BACK]
-    ids = by_z(ids_ref[...])
-    found = jnp.zeros((TOK, 8), F32)
+    by_lane = router.T
+    rows = []
     for k in range(8):
-        hit = ids[:, k : k + 1] == iota((TOK, 128), 1)
-        value = jnp.sum(jnp.where(hit, router, 0.0), axis=1, keepdims=True)
-        found = jnp.where(iota((TOK, 8), 1) == k, value, found)
-    out_prob[...] = (found / probs_ref[...].astype(F32)).astype(BF)
-
-    grad_copy(1, -sgn).wait()
-    grad_copy(2, sgn).wait()
+        hit = ids_t[k : k + 1, :] == iota((128, TOK), 0)
+        rows.append(jnp.sum(jnp.where(hit, by_lane, 0.0), axis=0, keepdims=True))
+    out_prob[...] = (jnp.concatenate(rows, axis=0) / probs_t).astype(BF)
+
+    for m in (0, 1):
+        grad_copy(1, m, -sgn).wait()
+        grad_copy(2, m, sgn).wait()
 
     def add_grads(n):
         at = rows16(n * 32, 32)
@@ -465,25 +530,31 @@
 
     loop(0, 512 // 32, add_grads)
 
-    loop(1, 8, lambda i: meta_copy(i).wait_send())
-    loop(1, 8, lambda i: over_copy(i).wait_send())
-    loop(1, 8, lambda i: back_over_copy(i).wait_send())
     loop(1, 8, lambda i: back_copy(0, i).wait_send())
 
-    def drain(pos):
-        loop(1, 8, lambda i: row_copy(pos, 0, i).wait_send())
-        loop(1, 8, lambda i: row_copy(pos, 1, i).wait_send())
-
-    loop(0, NZ, drain)
-
-    def drain_ring(pos):
-        def piece(h):
-            ag_copy(tok_ref, pos, h, sgn).wait_send()
-            sum_copy(pos, h, sgn).wait_send()
-
-        loop(0, 2, piece)
-
-    loop(1, 8, drain_ring)
+    def drain_sums(pos):
+        sum_copy(pos, 0, sgn).wait_send()
+        sum_copy(pos, 1, sgn).wait_send()
+
+    loop(1, 8, drain_sums)
+
+
+def copy_out(*refs):
+    sources, targets, held, sems = refs[:4], refs[4:8], refs[8:12], refs[12]
+    parts = [(0, 0, 128), (1, 0, 8)] + [(2, k * 128, 128) for k in range(4)] + [(3, k * 256, 256) for k in range(2)]
+
+    def copy(at, which, a, b):
+        n, start, count = parts[at]
+        rows = pl.ds(start, count)
+        return pltpu.make_async_copy(a[n].at[rows], b[n].at[rows], sems.at[which, at])
+
+    for at in range(len(parts)):
+        copy(at, 0, sources, held).start()
+    for at in range(len(parts)):
+        copy(at, 0, sources, held).wait()
+        copy(at, 1, held, targets).start()
+    for at in range(len(parts)):
+        copy(at, 1, held, targets).wait()
 
 
 def on_device(tokens, out_grad, expert_ids, route_probs, w_gate_up, w_down):
@@ -493,7 +564,7 @@
         kernel,
         out_shape=(
             jax.ShapeDtypeStruct((TOK, D), BF),
-            jax.ShapeDtypeStruct((TOK, 8), BF),
+            jax.ShapeDtypeStruct((8, TOK), BF),
             jax.ShapeDtypeStruct((512, 2 * FF), F32),
             jax.ShapeDtypeStruct((512, FF), F32),
         ),
@@ -504,6 +575,8 @@
             vm((D, FF), BF),
             vm((NZ, 16, TOK), F32),
             vm((NZ, 16, TOK), F32),
+            vm((16, D), BF),
+            vm((16, D), BF),
             vm((2, NZ, MAIN + 16, TOK), BF),
             vm((NZ, TOK, MAIN), BF),
             vm((NZ, TOK, 128), BF),
@@ -527,6 +600,7 @@
             vm((2, 512, 3 * FF), BF),
             vm((3, 512, 3 * FF), BF),
             dma((2,)),
+            dma((2,)),
             dma((8,)), dma((8,)),
             dma((7, 2)), dma((7, 2)),
             dma((16, 8)), dma((16, 8)),
@@ -534,15 +608,25 @@
             dma((8, 8)), dma((8, 8)),
             dma((8,)), dma((8,)),
             dma((7, 2)), dma((7, 2)),
-            dma((3,)), dma((3,)),
+            dma((3, 2)), dma((3, 2)),
         ],
         compiler_params=pltpu.CompilerParams(
             collective_id=0, has_side_effects=True, vmem_limit_bytes=62 * 2**20
         ),
         cost_estimate=pl.CostEstimate(flops=15 * 10**9, bytes_accessed=10**7, transcendentals=10**6),
         name="routed_backward",
-    )(tokens, out_grad, expert_ids, route_probs, w_gate_up[0], w_down[0])
-    return token_grad, prob_grad, grad_gu[None], grad_dn[None]
+    )(tokens, out_grad, expert_ids.T, route_probs.T, w_gate_up[0], w_down[0])
+    results = (token_grad, prob_grad, grad_gu, grad_dn)
+    anywhere = pl.BlockSpec(memory_space=pltpu.HBM)
+    token_grad, prob_grad, grad_gu, grad_dn = pl.pallas_call(
+        copy_out,
+        out_shape=tuple(jax.ShapeDtypeStruct(r.shape, r.dtype) for r in results),
+        in_specs=[anywhere] * 4,
+        out_specs=(anywhere,) * 4,
+        scratch_shapes=[vm(r.shape, r.dtype) for r in results] + [dma((2, 8))],
+        name="results",
+    )(*results)
+    return token_grad, prob_grad.T, grad_gu[None], grad_dn[None]
 
 
 def solution(mesh):

time: 215 us -> 186 us (0.87)
  Pallas kernels: 204 us -> 185 us
  local copies, waits for them, and re-layouts: 9.71 us -> 0 us
    pallas_call x1, Pallas kernels: 204 us -> 182 us  [on_device(): pl.pallas_call(kernel, out_shape=(jax.ShapeDtypeStruct((TOK, D), BF), jax...]
    unnamed x8 -> x0, local copies, waits for them, and re-layouts: 9.71 us -> none
    pallas_call x0 -> x1, Pallas kernels: none -> 2.75 us  [on_device(): pl.pallas_call(copy_out, out_shape=tuple((jax.ShapeDtypeStruct(r.shape, r...]
where the time goes in v2:
time: 186 us; the launch traced here: 185 us
  Pallas kernels  185 us (99%)
    pallas_call x1, Pallas kernels, on_device(): pl.pallas_call(kernel, out_shape=(jax.ShapeDtypeStruct((TOK, D), BF), jax...  182 us

profile of v2, /device:TPU:1, one launch (start us, length us, event | category | flops | bytes accessed | tf_op | source)
XLA Modules:
  0.0 185.5 jit_solution(18094326432499265999)
XLA Ops:
  0.6 182.1 %routed_backward.1 = (bf16[128,2048]{1,0:T(8,128)(2,1)}, bf16[8,128]{1,0:T(8,128)(2,1)}, f32[512,768]{1,0:T(8,128)}, f32[512,384]{1,0:T(8,128)}) custom-call(bf16[128,2048]{1,0:T(8,128)(2,1)} %tok_ref.1, bf16[128,2048]{1,0:T(8,128)(2,1)} %dy_ref.1, s32[8,128]{1,0:T(8,128)} %bitcast.11, bf16[8,128]{1,0:T(8,128)(2,1)} %bitcast.12, bf16[2048,768]{1,0:T(8,128)(2,1)} %bitcast.7, ...), custom_call_target="tpu_custom_call" | custom-call | flops 15000000512 | bytes 10000000 | tf_op jit(solution)/shard_map/routed_backward/pallas_call | solution.py:563
  182.7 2.8 %results.1 = (bf16[128,2048]{1,0:T(8,128)(2,1)}, bf16[8,128]{1,0:T(8,128)(2,1)}, f32[512,768]{1,0:T(8,128)}, f32[512,384]{1,0:T(8,128)}) custom-call(bf16[128,2048]{1,0:T(8,128)(2,1)} %get-tuple-element.12.refs_0_, bf16[8,128]{1,0:T(8,128)(2,1)} %get-tuple-element.13.refs_1_, f32[512,768]{1,0:T(8,128)} %get-tuple-element.14.refs_2_, ...), custom_call_target="tpu_custom_call" | custom-call | tf_op jit(solution)/shard_map/results/pallas_call | solution.py:621

commit v3 on v2

--- a/solution.py
+++ b/solution.py
@@ -19,8 +19,6 @@
 SLOT = 16
 MAIN = COL * SLOT
 ROWS = NZ * MAIN + COL * NZ
-BACK = D + 128
-OVB = D // 2 + 128
 OVER = (NZ - 1) * MAIN
 CW = 256
 
@@ -45,6 +43,10 @@
     return pl.ds(pl.multiple_of(n * width, width), width)
 
 
+def wide(n):
+    return slice(n * 1024, n * 1024 + 1024)
+
+
 def rows16(start, count):
     return pl.ds(pl.multiple_of(start, 16), count)
 
@@ -54,24 +56,26 @@
 
 
 def kernel(
-    tok_ref, dy_ref, ids_ref, probs_ref, wgu_hbm, wdn_hbm,
+    tok_hbm, dy_hbm, ids_ref, probs_ref, wgu_hbm, wdn_hbm,
     out_tok, out_prob, out_gu, out_dn,
-    wgu, wdn, meta_own, meta_all, far, far_in, sel, sel_t, sov_t, blk, sendbuf, ovf32, ovsend, ovrecv,
-    xs, gu, hg, hbuf, dgu, retbuf, retrecv, retov, retovr, rovf, tf, rsr, gsend, grecv,
-    w_sem, far_sem, meta_s, meta_r, ag_s, ag_r, d_s, d_r, ov_s, ov_r, r_s, r_r, ro_s, ro_r, rs_s, rs_r, g_s, g_r,
+    tok_ref, dy_ref, wgu, wdn, meta_own, meta_all, far, far_in, sel, sel_t, sov_t, blk, sendbuf, ovf32, ovsend, ovrecv,
+    xs, gu, hg, hbuf, dgu, retbuf, retrecv, retov, retovr, rovf, tf, rsr, gsend, grecv, qbuf, qin, gq, gall,
+    w_sem, far_sem, meta_s, meta_r, ag_s, ag_r, d_s, d_r, ov_s, ov_r, r_s, r_r, ro_s, ro_r, rs_s, rs_r, g_s, g_r, q_s, q_r, p_s, p_r,
 ):
     e = lax.axis_index("expert")
     x = lax.axis_index("dp")
     y, z, c = e // 16, (e // 2) % 8, e % 2
     s = y * 2 + c
     sgn = 1 - 2 * c
-    expert_lane = z * 8 + s
 
     def zdev(k):
         return ((y * 8 + (z + k + 8) % 8) * 2 + c, x)
 
     def coldev(t):
         return (((t // 2) * 8 + z) * 2 + t % 2, x)
+
+    other = [(s + i) % 8 for i in range(8)]
+    other_dev = [coldev(t) for t in other]
 
     def xdev(k):
         return (e, (x + k + 4) % 4)
@@ -100,13 +104,13 @@
         return remote(src, blk.at[pos - 1, p], ag_s.at[pos - 1, p], ag_r.at[pos - 1, p], zdev(k))
 
     def row_copy(pos, p, i):
-        t = (s + i) % 8
+        t, dev = (other[i], other_dev[i]) if isinstance(i, int) else (s, coldev((s + i) % 8))
         return remote(
             sendbuf.at[pos, p, rows16(t * SLOT, SLOT)],
             xs.at[p, rows16(base(pos) + s * SLOT, SLOT)],
             d_s.at[pos * 2 + p, i],
             d_r.at[pos * 2 + p, i],
-            coldev(t),
+            dev,
         )
 
     def over_copy(i):
@@ -116,13 +120,13 @@
         )
 
     def back_copy(pos, i):
-        t = (s + i) % 8
+        t, dev = (other[i], other_dev[i]) if isinstance(i, int) else (s, coldev((s + i) % 8))
         return remote(
             retbuf.at[rows16(base(pos) + t * SLOT, SLOT)],
             retrecv.at[pos, rows16(s * SLOT, SLOT)],
             r_s.at[pos, i],
             r_r.at[pos, i],
-            coldev(t),
+            dev,
         )
 
     def back_over_copy(i):
@@ -149,13 +153,16 @@
             xdev(k),
         )
 
+    def q_copy(i):
+        t = (s + i) % 8
+        return remote(qbuf.at[rows16(t * 16, 16)], qin.at[rows16(s * 16, 16)], q_s.at[i], q_r.at[i], coldev(t))
+
+    def p_copy(pos):
+        k = -sgn * ((pos + 1) // 2) if pos % 2 else sgn * (pos // 2)
+        return remote(gq.at[pos], gall.at[z], p_s.at[pos], p_r.at[pos], zdev(k))
+
     def far_copy():
         return remote(far, far_in, far_sem.at[0], far_sem.at[1], zdev(4))
-
-    w_gu_copy = pltpu.make_async_copy(wgu_hbm, wgu, w_sem.at[0])
-    w_dn_copy = pltpu.make_async_copy(wdn_hbm, wdn, w_sem.at[1])
-    w_gu_copy.start()
-    w_dn_copy.start()
 
     barrier = pltpu.get_barrier_semaphore()
     for i in range(1, 8):
@@ -163,6 +170,16 @@
         pl.semaphore_signal(barrier, inc=1, device_id=coldev((s + i) % 8), device_id_type=MESH)
     for k in (-1, 1):
         pl.semaphore_signal(barrier, inc=1, device_id=xdev(k), device_id_type=MESH)
+    x_copy = pltpu.make_async_copy(tok_hbm, tok_ref, w_sem.at[2])
+    dy_copy = pltpu.make_async_copy(dy_hbm, dy_ref, w_sem.at[3])
+    x_copy.start()
+    dy_copy.start()
+    w_gu_copy = pltpu.make_async_copy(wgu_hbm, wgu, w_sem.at[0])
+    w_dn_copy = pltpu.make_async_copy(wdn_hbm, wdn, w_sem.at[1])
+    w_gu_copy.start()
+    w_dn_copy.start()
+    qbuf[...] = jnp.zeros((192, 128), F32)
+
     def by_z(ids):
         return ((ids // 2) % 8) * 8 + (ids // 16) * 2 + ids % 2
 
@@ -201,36 +218,32 @@
         sov_t[pos] = wide.T.astype(BF)
 
     def pick(pos, p, ref):
-        def column(n):
-            got = dot(sel[p, pos], ref[:, tile(n)])
-            sendbuf[pos, p, :, tile(n)] = got[:MAIN].astype(BF)
-            ovf32[p, pl.ds(pl.multiple_of(pos * 8, 8), 8), tile(n)] = got[MAIN : MAIN + 8]
-
-        loop(0, D // CW, column)
+        for n in (0, 1):
+            got = dot(sel[p, pos], ref[:, wide(n)])
+            sendbuf[pos, p, :, wide(n)] = got[:MAIN].astype(BF)
+            ovf32[p, pl.ds(pl.multiple_of(pos * 8, 8), 8), wide(n)] = got[MAIN : MAIN + 8]
 
     def send(pos, p):
-        loop(1, 8, lambda i: row_copy(pos, p, i).start())
+        for i in range(1, 8):
+            row_copy(pos, p, i).start()
         xs[p, rows16(base(pos) + s * SLOT, SLOT), :] = sendbuf[pos, p, rows16(s * SLOT, SLOT), :]
 
+    def await_half(pos, p):
+        for i in range(1, 8):
+            row_copy(pos, p, i).wait_recv()
+
     def await_rows(pos):
-        loop(1, 8, lambda i: row_copy(pos, 0, i).wait_recv())
-        loop(1, 8, lambda i: row_copy(pos, 1, i).wait_recv())
-
-    def expert(row0, count):
+        await_half(pos, 0)
+        await_half(pos, 1)
+
+    def expert(row0, count, places, between=lambda: None):
         rows = rows16(row0, count)
-
-        def first(n):
-            gu[0:count, tile(n)] = dot(xs[0, rows, :], wgu[:, tile(n)])
-
-        loop(0, 2 * FF // CW, first)
-
-        def second(n):
-            hg[0:count, tile(n, 128)] = dot(xs[1, rows, :], wdn[:, tile(n, 128)])
-
-        loop(0, FF // 128, second)
-
-        def middle(n):
-            part, whole = rows16(n * 32, 32), rows16(row0 + n * 32, 32)
+        gu[0:count, :] = dot(xs[0, rows, :], wgu[...])
+        between()
+        hg[0:count, :] = dot(xs[1, rows, :], wdn[...])
+
+        def middle(n, place, lane):
+            part, whole = rows16(n * 64, 64), rows16(row0 + n * 64, 64)
             gate, up, grad = gu[part, 0:FF], gu[part, FF : 2 * FF], hg[part, :]
             sig = jax.nn.sigmoid(gate)
             silu = gate * sig
@@ -239,43 +252,51 @@
             dgu[whole, 0:FF] = (grad * up * sig * (1.0 + gate * (1.0 - sig))).astype(BF)
             dgu[whole, FF : 2 * FF] = (grad * silu).astype(BF)
             router = jnp.sum(grad * act.astype(F32), axis=1, keepdims=True)
-            retbuf[whole, D:BACK] = jnp.where(iota((32, 128), 1) == expert_lane, router, 0.0).astype(BF)
-
-        loop(0, count // 32, middle)
+            at = pl.ds(pl.multiple_of(place, 16), 64)
+            qbuf[at, :] = qbuf[at, :] + jnp.where(iota((64, 128), 1) == lane, router, 0.0)
+
+        for lo, hi, place in places:
+            loop(lo, hi, lambda n, place=place: middle(n, *place(n)))
 
         def last(n):
-            retbuf[rows, tile(n)] = dot_nt(dgu[rows, :], wgu[tile(n), :]).astype(BF)
-
-        loop(0, D // CW, last)
+            retbuf[rows, tile(n, 512)] = dot_nt(dgu[rows, :], wgu[tile(n, 512), :]).astype(BF)
+
+        loop(0, D // 512, last)
 
     build(0, meta_own[z])
+    x_copy.wait()
     pick(0, 0, tok_ref)
+
+    pl.semaphore_wait(barrier, 16)
+
+    ag_copy(tok_ref, 1, 0, sgn).start()
+    ag_copy(tok_ref, 2, 0, -sgn).start()
+    send(0, 0)
+    loop(1, 8, lambda i: meta_copy(i).start())
+    dy_copy.wait()
+    ag_copy(dy_ref, 1, 1, sgn).start()
+    ag_copy(dy_ref, 2, 1, -sgn).start()
     pick(0, 1, dy_ref)
+    send(0, 1)
+
     opposite = meta_own[(z + 4) % 8]
     nobody = jnp.zeros((8, TOK), F32)
     far_one = jnp.concatenate([jnp.where(opposite[0:8] == float(SLOT), 1.0, 0.0), nobody], axis=0).astype(BF)
     far_weight = jnp.concatenate([nobody, jnp.where(opposite[0:8] == float(SLOT), opposite[8:16], 0.0)], axis=0).astype(BF)
 
-    def far_rows(n):
-        far[:, tile(n)] = (dot(far_one, tok_ref[:, tile(n)]) + dot(far_weight, dy_ref[:, tile(n)])).astype(BF)
-
-    loop(0, D // CW, far_rows)
-
-    pl.semaphore_wait(barrier, 16)
-
-    ag_copy(tok_ref, 1, 0, sgn).start()
-    ag_copy(tok_ref, 2, 0, -sgn).start()
-    send(0, 0)
-    loop(1, 8, lambda i: meta_copy(i).start())
-    ag_copy(dy_ref, 1, 1, sgn).start()
-    ag_copy(dy_ref, 2, 1, -sgn).start()
-    send(0, 1)
+    for n in (0, 1):
+        far[:, wide(n)] = (dot(far_one, tok_ref[:, wide(n)]) + dot(far_weight, dy_ref[:, wide(n)])).astype(BF)
     far_copy().start()
     w_gu_copy.wait()
     w_dn_copy.wait()
 
     r128, c64 = iota((128, 64), 0), iota((128, 64), 1)
     r64, c128 = iota((64, 128), 0), iota((64, 128), 1)
+
+    def pair(pos):
+        await_rows(pos)
+        await_rows(pos + 1)
+        expert(pos * MAIN, 2 * MAIN, [(0, 4, lambda n: ((n % 2) * 64, (pos + n // 2) * 8 + s))])
 
     def turn(d):
         odd, even = 2 * d - 1, 2 * d
@@ -289,6 +310,10 @@
             build(even, meta_all[down_at])
 
         def piece(p):
+            @pl.when((p == 1) & (d >= 2) & (d < 4))
+            def _():
+                pair(2 * d - 4)
+
             ag_copy(tok_ref, odd, p, sgn).wait_recv()
 
             @pl.when(d < 4)
@@ -319,56 +344,52 @@
             where_of = c64 == (r128 % 8) * 8 + r128 // 16
             first, second = mask((r128 % 16 < 8) & where_of), mask((r128 % 16 >= 8) & where_of)
 
-            def column(n):
-                a, b = ovf32[0, :, tile(n)].astype(BF), ovf32[1, :, tile(n)].astype(BF)
-                ovsend[:, tile(n)] = (dot(first, a) + dot(second, b)).astype(BF)
-
-            loop(0, D // CW, column)
+            for n in (0, 1):
+                a, b = ovf32[0, :, wide(n)].astype(BF), ovf32[1, :, wide(n)].astype(BF)
+                ovsend[:, wide(n)] = (dot(first, a) + dot(second, b)).astype(BF)
             loop(1, 8, lambda i: over_copy(i).start())
             ovrecv[rows16(s * 16, 16), :] = ovsend[rows16(s * 16, 16), :]
 
-        @pl.when(d >= 2)
-        def _():
-            await_rows(2 * d - 4)
-            await_rows(2 * d - 3)
-            expert((2 * d - 4) * MAIN, 2 * MAIN)
 
     loop(1, 5, turn)
 
+    pair(4)
     await_rows(6)
     loop(1, 8, lambda i: over_copy(i).wait_recv())
     take_lo = mask(c128 == (r64 // 8) * 16 + r64 % 8)
     take_hi = mask(c128 == (r64 // 8) * 16 + 8 + r64 % 8)
 
-    def unpack(n):
-        got = ovrecv[:, tile(n)]
-        xs[0, OVER : OVER + COL * NZ, tile(n)] = dot(take_lo, got).astype(BF)
-        xs[1, OVER : OVER + COL * NZ, tile(n)] = dot(take_hi, got).astype(BF)
-
-    loop(0, D // CW, unpack)
-    expert(6 * MAIN, MAIN + COL * NZ)
+    for n in (0, 1):
+        got = ovrecv[:, wide(n)]
+        xs[0, OVER : OVER + COL * NZ, wide(n)] = dot(take_lo, got).astype(BF)
+        xs[1, OVER : OVER + COL * NZ, wide(n)] = dot(take_hi, got).astype(BF)
+    expert(
+        6 * MAIN,
+        MAIN + COL * NZ,
+        [(0, 2, lambda n: (n * 64, 48 + s)), (2, 3, lambda n: (n * 64, 64 + s))],
+    )
 
     put_lo = mask((r128 % 16 < 8) & (c64 == (r128 // 16) * 8 + r128 % 16))
     put_hi = mask((r128 % 16 >= 8) & (c64 == (r128 // 16) * 8 + r128 % 16 - 8))
     over_rows = pl.ds(OVER, COL * NZ)
 
-    def pack(n):
-        lo, hi = retbuf[over_rows, tile(n)], retbuf[over_rows, tile(n + 4)]
-        retov[:, tile(n)] = (dot(put_lo, lo) + dot(put_hi, hi)).astype(BF)
-
-    loop(0, D // 2 // CW, pack)
-    retov[:, D // 2 : OVB] = dot(put_lo, retbuf[over_rows, D:BACK]).astype(BF)
+    retov[...] = (dot(put_lo, retbuf[over_rows, wide(0)]) + dot(put_hi, retbuf[over_rows, wide(1)])).astype(BF)
     loop(1, 8, lambda i: back_over_copy(i).start())
     retovr[rows16(s * 16, 16), :] = retov[rows16(s * 16, 16), :]
 
     def send_back(pos):
-        loop(1, 8, lambda i: back_copy(pos, i).start())
+        for i in range(1, 8):
+            back_copy(pos, i).start()
         retrecv[pos, rows16(s * SLOT, SLOT), :] = retbuf[rows16(base(pos) + s * SLOT, SLOT), :]
 
     send_back(6)
-    await_rows(7)
-    expert(base(7), MAIN)
+    await_half(7, 0)
+    expert(base(7), MAIN, [(0, 2, lambda n: (n * 64, 56 + s))], lambda: await_half(7, 1))
     send_back(7)
+    for t in range(8):
+        qbuf[t * 16 : t * 16 + 8, :] = qbuf[t * 16 : t * 16 + 8, :] + qbuf[MAIN + t * 8 : MAIN + t * 8 + 8, :]
+    loop(1, 8, lambda i: q_copy(i).start())
+    qin[rows16(s * 16, 16), :] = qbuf[rows16(s * 16, 16), :]
 
     def send_pair(k):
         send_back(4 - 2 * k)
@@ -408,27 +429,22 @@
 
     loop(1, 8, lambda i: back_over_copy(i).wait_recv())
 
-    def unpack_back(n):
-        got = retovr[:, tile(n)]
-        rovf[0:64, tile(n)] = dot(take_lo, got).astype(BF)
-        rovf[0:64, tile(n + 4)] = dot(take_hi, got).astype(BF)
-
-    loop(0, D // 2 // CW, unpack_back)
-    rovf[0:64, D:BACK] = dot(take_lo, retovr[:, D // 2 : OVB]).astype(BF)
-    rovf[64:128, :] = jnp.zeros((64, BACK), BF)
+    got_back = retovr[...]
+    rovf[0:64, wide(0)] = dot(take_lo, got_back).astype(BF)
+    rovf[0:64, wide(1)] = dot(take_hi, got_back).astype(BF)
+    rovf[64:128, :] = jnp.zeros((64, D), BF)
 
     def combine(pos):
-        loop(1, 8, lambda i: back_copy(pos, i).wait_recv())
-
-        def column(n):
-            tf[:, tile(n)] = dot(sel_t[pos], retrecv[pos, :, tile(n)]) + dot(sov_t[pos], rovf[:, tile(n)])
-
-        loop(0, D // CW, column)
-        tf[:, D:BACK] = dot(sel_t[pos], retrecv[pos, :, D:BACK]) + dot(sov_t[pos], rovf[:, D:BACK])
+        for i in range(1, 8):
+            back_copy(pos, i).wait_recv()
+
+        for n in (0, 1):
+            tf[:, wide(n)] = dot(sel_t[pos], retrecv[pos, :, wide(n)]) + dot(sov_t[pos], rovf[:, wide(n)])
 
     def pass_on(pos, k, has_more):
         combine(pos)
-        loop(1, 8, lambda i: back_copy(pos, i).wait_send())
+        for i in range(1, 8):
+            back_copy(pos, i).wait_send()
 
         def piece(h):
             @pl.when(has_more)
@@ -454,6 +470,15 @@
 
         loop(0, 2, piece)
 
+    def add_grads(slot):
+        def part(n):
+            at = rows16(n * 32, 32)
+            more = grecv[slot, at, :].astype(F32)
+            out_gu[at, :] = out_gu[at, :] + more[:, 0 : 2 * FF]
+            out_dn[at, :] = out_dn[at, :] + more[:, 2 * FF :]
+
+        loop(0, 512 // 32, part)
+
     def drain():
         far_copy().wait_send()
         loop(1, 8, lambda i: meta_copy(i).wait_send())
@@ -472,6 +497,23 @@
 
         loop(1, 8, drain_ring)
 
+    def routers():
+        loop(1, 8, lambda i: q_copy(i).wait_recv())
+        held = qin[0:16, :]
+        for o in range(1, 8):
+            held = held + qin[o * 16 : o * 16 + 16, :]
+        for pos in range(NZ):
+            one = sel[0, pos, :, :].astype(F32)
+            rows = []
+            for o in range(8):
+                value = held[:, pos * 8 + o : pos * 8 + o + 1]
+                row = jnp.sum(one[o * 16 : o * 16 + 16] * value, axis=0, keepdims=True)
+                rows.append(row + one[MAIN + o : MAIN + o + 1] * held[pos : pos + 1, 64 + o : 65 + o])
+            gq[pos] = jnp.concatenate(rows, axis=0)
+        for pos in range(1, NZ):
+            p_copy(pos).start()
+        gall[z] = gq[0]
+
     def back_turn(k):
         @pl.when(k < 3)
         def _():
@@ -479,13 +521,9 @@
 
         pass_on(7 - 2 * k, -sgn, k > 0)
 
-        @pl.when(k == 0)
+        @pl.when(k < 2)
         def _():
-            drain()
-
-        @pl.when((k == 1) | (k == 2))
-        def _():
-            m = k - 1
+            m = k
             grad_copy(0, m, sgn).wait()
 
             def emit(a, b):
@@ -496,6 +534,20 @@
             weight_grad((x + sgn + 4) % 4, m, emit)
             grad_copy(2, m, sgn).start()
 
+        @pl.when(k == 0)
+        def _():
+            routers()
+
+        @pl.when(k == 1)
+        def _():
+            drain()
+
+        @pl.when(k == 2)
+        def _():
+            for m in (0, 1):
+                grad_copy(1, m, -sgn).wait()
+            add_grads(1)
+
     loop(0, 4, back_turn)
 
     combine(0)
@@ -506,31 +558,24 @@
     def finish(n):
         at = rows16(n * 16, 16)
         total = tf[at, :] + rsr[0, at, :].astype(F32) + rsr[1, at, :].astype(F32)
-        out_tok[at, :] = total[:, 0:D].astype(BF)
-        tf[at, D:BACK] = total[:, D:BACK]
+        out_tok[at, :] = total.astype(BF)
 
     loop(0, TOK // 16, finish)
-    router = tf[:, D:BACK]
-    by_lane = router.T
+    for pos in range(1, NZ):
+        p_copy(pos).wait()
+    by_lane = gall[...].reshape(64, TOK)
     rows = []
     for k in range(8):
-        hit = ids_t[k : k + 1, :] == iota((128, TOK), 0)
+        hit = ids_t[k : k + 1, :] == lane_of
         rows.append(jnp.sum(jnp.where(hit, by_lane, 0.0), axis=0, keepdims=True))
     out_prob[...] = (jnp.concatenate(rows, axis=0) / probs_t).astype(BF)
 
     for m in (0, 1):
-        grad_copy(1, m, -sgn).wait()
         grad_copy(2, m, sgn).wait()
-
-    def add_grads(n):
-        at = rows16(n * 32, 32)
-        more = grecv[1, at, :].astype(F32) + grecv[2, at, :].astype(F32)
-        out_gu[at, :] = out_gu[at, :] + more[:, 0 : 2 * FF]
-        out_dn[at, :] = out_dn[at, :] + more[:, 2 * FF :]
-
-    loop(0, 512 // 32, add_grads)
+    add_grads(2)
 
     loop(1, 8, lambda i: back_copy(0, i).wait_send())
+    loop(1, 8, lambda i: q_copy(i).wait_send())
 
     def drain_sums(pos):
         sum_copy(pos, 0, sgn).wait_send()
@@ -568,9 +613,11 @@
             jax.ShapeDtypeStruct((512, 2 * FF), F32),
             jax.ShapeDtypeStruct((512, FF), F32),
         ),
-        in_specs=[inside] * 4 + [pl.BlockSpec(memory_space=pl.ANY)] * 2,
+        in_specs=[pl.BlockSpec(memory_space=pl.ANY)] * 2 + [inside] * 2 + [pl.BlockSpec(memory_space=pl.ANY)] * 2,
         out_specs=(inside,) * 4,
         scratch_shapes=[
+            vm((TOK, D), BF),
+            vm((TOK, D), BF),
             vm((D, 2 * FF), BF),
             vm((D, FF), BF),
             vm((NZ, 16, TOK), F32),
@@ -590,16 +637,20 @@
             vm((320, FF), F32),
             vm((ROWS, FF), BF),
             vm((ROWS, 2 * FF), BF),
-            vm((ROWS, BACK), BF),
-            vm((NZ, MAIN, BACK), BF),
-            vm((128, OVB), BF),
-            vm((128, OVB), BF),
-            vm((128, BACK), BF),
-            vm((TOK, BACK), F32),
-            vm((NZ - 1, TOK, BACK), BF),
+            vm((ROWS, D), BF),
+            vm((NZ, MAIN, D), BF),
+            vm((128, D // 2), BF),
+            vm((128, D // 2), BF),
+            vm((128, D), BF),
+            vm((TOK, D), F32),
+            vm((NZ - 1, TOK, D), BF),
             vm((2, 512, 3 * FF), BF),
             vm((3, 512, 3 * FF), BF),
-            dma((2,)),
+            vm((192, 128), F32),
+            vm((128, 128), F32),
+            vm((NZ, 8, TOK), F32),
+            vm((NZ, 8, TOK), F32),
+            dma((4,)),
             dma((2,)),
             dma((8,)), dma((8,)),
             dma((7, 2)), dma((7, 2)),
@@ -609,6 +660,8 @@
             dma((8,)), dma((8,)),
             dma((7, 2)), dma((7, 2)),
             dma((3, 2)), dma((3, 2)),
+            dma((8,)), dma((8,)),
+            dma((8,)), dma((8,)),
         ],
         compiler_params=pltpu.CompilerParams(
             collective_id=0, has_side_effects=True, vmem_limit_bytes=62 * 2**20

time: 186 us -> 179 us (0.962)
  Pallas kernels: 185 us -> 178 us
    pallas_call x1, Pallas kernels: 182 us -> 175 us  [on_device(): pl.pallas_call(kernel, out_shape=(jax.ShapeDtypeStruct((TOK, D), BF), jax...]
where the time goes in v3:
time: 179 us; the launch traced here: 178 us
  Pallas kernels  178 us (99%)
    pallas_call x1, Pallas kernels, on_device(): pl.pallas_call(kernel, out_shape=(jax.ShapeDtypeStruct((TOK, D), BF), jax...  175 us

profile of v3, /device:TPU:1, one launch (start us, length us, event | category | flops | bytes accessed | tf_op | source)
XLA Modules:
  0.0 178.3 jit_solution(5201925446933552893)
XLA Ops:
  0.6 174.8 %routed_backward.1 = (bf16[128,2048]{1,0:T(8,128)(2,1)}, bf16[8,128]{1,0:T(8,128)(2,1)}, f32[512,768]{1,0:T(8,128)}, f32[512,384]{1,0:T(8,128)}) custom-call(bf16[128,2048]{1,0:T(8,128)(2,1)} %tok_hbm.1, bf16[128,2048]{1,0:T(8,128)(2,1)} %dy_hbm.1, s32[8,128]{1,0:T(8,128)} %bitcast.11, bf16[8,128]{1,0:T(8,128)(2,1)} %bitcast.12, bf16[2048,768]{1,0:T(8,128)(2,1)} %bitcast.7, ...), custom_call_target="tpu_custom_call" | custom-call | flops 15000000512 | bytes 10000000 | tf_op jit(solution)/shard_map/routed_backward/pallas_call | solution.py:608
  175.4 2.8 %results.1 = (bf16[128,2048]{1,0:T(8,128)(2,1)}, bf16[8,128]{1,0:T(8,128)(2,1)}, f32[512,768]{1,0:T(8,128)}, f32[512,384]{1,0:T(8,128)}) custom-call(bf16[128,2048]{1,0:T(8,128)(2,1)} %get-tuple-element.12.refs_0_, bf16[8,128]{1,0:T(8,128)(2,1)} %get-tuple-element.13.refs_1_, f32[512,768]{1,0:T(8,128)} %get-tuple-element.14.refs_2_, ...), custom_call_target="tpu_custom_call" | custom-call | tf_op jit(solution)/shard_map/results/pallas_call | solution.py:674

commit v4 on v3

--- a/solution.py
+++ b/solution.py
@@ -57,8 +57,8 @@
 
 def kernel(
     tok_hbm, dy_hbm, ids_ref, probs_ref, wgu_hbm, wdn_hbm,
-    out_tok, out_prob, out_gu, out_dn,
-    tok_ref, dy_ref, wgu, wdn, meta_own, meta_all, far, far_in, sel, sel_t, sov_t, blk, sendbuf, ovf32, ovsend, ovrecv,
+    out_tok, out_prob, gu_hbm, dn_hbm,
+    out_gu, out_dn, own, wgu, wdn, meta_own, meta_all, far, far_in, sel, sel_t, sov_t, blk, sendbuf, ovf32, ovsend, ovrecv,
     xs, gu, hg, hbuf, dgu, retbuf, retrecv, retov, retovr, rovf, tf, rsr, gsend, grecv, qbuf, qin, gq, gall,
     w_sem, far_sem, meta_s, meta_r, ag_s, ag_r, d_s, d_r, ov_s, ov_r, r_s, r_r, ro_s, ro_r, rs_s, rs_r, g_s, g_r, q_s, q_r, p_s, p_r,
 ):
@@ -107,9 +107,9 @@
         t, dev = (other[i], other_dev[i]) if isinstance(i, int) else (s, coldev((s + i) % 8))
         return remote(
             sendbuf.at[pos, p, rows16(t * SLOT, SLOT)],
-            xs.at[p, rows16(base(pos) + s * SLOT, SLOT)],
-            d_s.at[pos * 2 + p, i],
-            d_r.at[pos * 2 + p, i],
+            xs.at[p // 2, rows16(base(pos) + s * SLOT, SLOT), tile(p % 2, 1024)],
+            d_s.at[pos * 4 + p, i],
+            d_r.at[pos * 4 + p, i],
             dev,
         )
 
@@ -170,10 +170,12 @@
         pl.semaphore_signal(barrier, inc=1, device_id=coldev((s + i) % 8), device_id_type=MESH)
     for k in (-1, 1):
         pl.semaphore_signal(barrier, inc=1, device_id=xdev(k), device_id_type=MESH)
-    x_copy = pltpu.make_async_copy(tok_hbm, tok_ref, w_sem.at[2])
-    dy_copy = pltpu.make_async_copy(dy_hbm, dy_ref, w_sem.at[3])
-    x_copy.start()
-    dy_copy.start()
+    own_copies = [
+        pltpu.make_async_copy((tok_hbm, tok_hbm, dy_hbm, dy_hbm)[p].at[:, wide(p % 2)], own.at[p], w_sem.at[2 + p])
+        for p in range(4)
+    ]
+    for one_copy in own_copies:
+        one_copy.start()
     w_gu_copy = pltpu.make_async_copy(wgu_hbm, wgu, w_sem.at[0])
     w_dn_copy = pltpu.make_async_copy(wdn_hbm, wdn, w_sem.at[1])
     w_gu_copy.start()
@@ -218,19 +220,19 @@
         sov_t[pos] = wide.T.astype(BF)
 
     def pick(pos, p, ref):
-        for n in (0, 1):
-            got = dot(sel[p, pos], ref[:, wide(n)])
-            sendbuf[pos, p, :, wide(n)] = got[:MAIN].astype(BF)
-            ovf32[p, pl.ds(pl.multiple_of(pos * 8, 8), 8), wide(n)] = got[MAIN : MAIN + 8]
+        got = dot(sel[p // 2, pos], ref[...])
+        sendbuf[pos, p] = got[:MAIN].astype(BF)
+        ovf32[p // 2, pl.ds(pl.multiple_of(pos * 8, 8), 8), tile(p % 2, 1024)] = got[MAIN : MAIN + 8]
 
     def send(pos, p):
         for i in range(1, 8):
             row_copy(pos, p, i).start()
-        xs[p, rows16(base(pos) + s * SLOT, SLOT), :] = sendbuf[pos, p, rows16(s * SLOT, SLOT), :]
+        xs[p // 2, rows16(base(pos) + s * SLOT, SLOT), tile(p % 2, 1024)] = sendbuf[pos, p, rows16(s * SLOT, SLOT), :]
 
     def await_half(pos, p):
         for i in range(1, 8):
-            row_copy(pos, p, i).wait_recv()
+            row_copy(pos, 2 * p, i).wait_recv()
+            row_copy(pos, 2 * p + 1, i).wait_recv()
 
     def await_rows(pos):
         await_half(pos, 0)
@@ -264,20 +266,24 @@
         loop(0, D // 512, last)
 
     build(0, meta_own[z])
-    x_copy.wait()
-    pick(0, 0, tok_ref)
+    own_copies[0].wait()
+    pick(0, 0, own.at[0])
 
     pl.semaphore_wait(barrier, 16)
 
-    ag_copy(tok_ref, 1, 0, sgn).start()
-    ag_copy(tok_ref, 2, 0, -sgn).start()
+    def own_ring(p):
+        ag_copy(own.at[p], 1, p, sgn).start()
+        ag_copy(own.at[p], 2, p, -sgn).start()
+
+    loop(1, 8, lambda i: meta_copy(i).start())
+    own_ring(0)
     send(0, 0)
-    loop(1, 8, lambda i: meta_copy(i).start())
-    dy_copy.wait()
-    ag_copy(dy_ref, 1, 1, sgn).start()
-    ag_copy(dy_ref, 2, 1, -sgn).start()
-    pick(0, 1, dy_ref)
-    send(0, 1)
+    for p in (1, 2, 3):
+        own_copies[p].wait()
+        own_ring(p)
+    for p in (1, 2, 3):
+        pick(0, p, own.at[p])
+        send(0, p)
 
     opposite = meta_own[(z + 4) % 8]
     nobody = jnp.zeros((8, TOK), F32)
@@ -285,7 +291,7 @@
     far_weight = jnp.concatenate([nobody, jnp.where(opposite[0:8] == float(SLOT), opposite[8:16], 0.0)], axis=0).astype(BF)
 
     for n in (0, 1):
-        far[:, wide(n)] = (dot(far_one, tok_ref[:, wide(n)]) + dot(far_weight, dy_ref[:, wide(n)])).astype(BF)
+        far[:, wide(n)] = (dot(far_one, own[n]) + dot(far_weight, own[2 + n])).astype(BF)
     far_copy().start()
     w_gu_copy.wait()
     w_dn_copy.wait()
@@ -310,11 +316,11 @@
             build(even, meta_all[down_at])
 
         def piece(p):
-            @pl.when((p == 1) & (d >= 2) & (d < 4))
+            @pl.when((p == 2) & (d >= 2) & (d < 4))
             def _():
                 pair(2 * d - 4)
 
-            ag_copy(tok_ref, odd, p, sgn).wait_recv()
+            ag_copy(own.at[p], odd, p, sgn).wait_recv()
 
             @pl.when(d < 4)
             def _():
@@ -325,7 +331,7 @@
 
             @pl.when(d < 4)
             def _():
-                ag_copy(tok_ref, even, p, -sgn).wait_recv()
+                ag_copy(own.at[p], even, p, -sgn).wait_recv()
 
                 @pl.when(d < 3)
                 def _():
@@ -334,7 +340,7 @@
                 pick(even, p, blk.at[even - 1, p])
                 send(even, p)
 
-        loop(0, 2, piece)
+        loop(0, 4, piece)
 
         @pl.when(d == 3)
         def _():
@@ -486,14 +492,13 @@
         loop(1, 8, lambda i: back_over_copy(i).wait_send())
 
         def drain_rows(pos):
-            loop(1, 8, lambda i: row_copy(pos, 0, i).wait_send())
-            loop(1, 8, lambda i: row_copy(pos, 1, i).wait_send())
+            loop(0, 4, lambda p: loop(1, 8, lambda i: row_copy(pos, p, i).wait_send()))
 
         loop(0, NZ, drain_rows)
 
         def drain_ring(pos):
-            ag_copy(tok_ref, pos, 0, sgn).wait_send()
-            ag_copy(tok_ref, pos, 1, sgn).wait_send()
+            for p in range(4):
+                ag_copy(own.at[p], pos, p, sgn).wait_send()
 
         loop(1, 8, drain_ring)
 
@@ -550,17 +555,14 @@
 
     loop(0, 4, back_turn)
 
-    combine(0)
-    for pos in (1, 2):
-        for h in (0, 1):
-            sum_copy(pos, h, sgn).wait_recv()
-
-    def finish(n):
-        at = rows16(n * 16, 16)
-        total = tf[at, :] + rsr[0, at, :].astype(F32) + rsr[1, at, :].astype(F32)
-        out_tok[at, :] = total.astype(BF)
-
-    loop(0, TOK // 16, finish)
+    for m in (0, 1):
+        grad_copy(2, m, sgn).wait()
+    add_grads(2)
+    gu_out = pltpu.make_async_copy(out_gu, gu_hbm, w_sem.at[0])
+    dn_out = pltpu.make_async_copy(out_dn, dn_hbm, w_sem.at[1])
+    gu_out.start()
+    dn_out.start()
+
     for pos in range(1, NZ):
         p_copy(pos).wait()
     by_lane = gall[...].reshape(64, TOK)
@@ -570,10 +572,17 @@
         rows.append(jnp.sum(jnp.where(hit, by_lane, 0.0), axis=0, keepdims=True))
     out_prob[...] = (jnp.concatenate(rows, axis=0) / probs_t).astype(BF)
 
-    for m in (0, 1):
-        grad_copy(2, m, sgn).wait()
-    add_grads(2)
-
+    combine(0)
+    for pos in (1, 2):
+        for h in (0, 1):
+            sum_copy(pos, h, sgn).wait_recv()
+
+    def finish(n):
+        at = rows16(n * 16, 16)
+        total = tf[at, :] + rsr[0, at, :].astype(F32) + rsr[1, at, :].astype(F32)
+        out_tok[at, :] = total.astype(BF)
+
+    loop(0, TOK // 16, finish)
     loop(1, 8, lambda i: back_copy(0, i).wait_send())
     loop(1, 8, lambda i: q_copy(i).wait_send())
 
@@ -582,6 +591,8 @@
         sum_copy(pos, 1, sgn).wait_send()
 
     loop(1, 8, drain_sums)
+    gu_out.wait()
+    dn_out.wait()
 
 
 def copy_out(*refs):
@@ -614,10 +625,11 @@
             jax.ShapeDtypeStruct((512, FF), F32),
         ),
         in_specs=[pl.BlockSpec(memory_space=pl.ANY)] * 2 + [inside] * 2 + [pl.BlockSpec(memory_space=pl.ANY)] * 2,
-        out_specs=(inside,) * 4,
+        out_specs=(inside,) * 2 + (pl.BlockSpec(memory_space=pl.ANY),) * 2,
         scratch_shapes=[
-            vm((TOK, D), BF),
-            vm((TOK, D), BF),
+            vm((512, 2 * FF), F32),
+            vm((512, FF), F32),
+            vm((4, TOK, D // 2), BF),
             vm((D, 2 * FF), BF),
             vm((D, FF), BF),
             vm((NZ, 16, TOK), F32),
@@ -627,8 +639,8 @@
             vm((2, NZ, MAIN + 16, TOK), BF),
             vm((NZ, TOK, MAIN), BF),
             vm((NZ, TOK, 128), BF),
-            vm((NZ - 1, 2, TOK, D), BF),
-            vm((NZ, 2, MAIN, D), BF),
+            vm((NZ - 1, 4, TOK, D // 2), BF),
+            vm((NZ, 4, MAIN, D // 2), BF),
             vm((2, 64, D), F32),
             vm((128, D), BF),
             vm((128, D), BF),
@@ -650,11 +662,11 @@
             vm((128, 128), F32),
             vm((NZ, 8, TOK), F32),
             vm((NZ, 8, TOK), F32),
-            dma((4,)),
+            dma((6,)),
             dma((2,)),
             dma((8,)), dma((8,)),
-            dma((7, 2)), dma((7, 2)),
-            dma((16, 8)), dma((16, 8)),
+            dma((7, 4)), dma((7, 4)),
+            dma((32, 8)), dma((32, 8)),
             dma((8,)), dma((8,)),
             dma((8, 8)), dma((8, 8)),
             dma((8,)), dma((8,)),

time: 179 us -> 177 us (0.989)
  Pallas kernels: 178 us -> 176 us
where the time goes in v4:
time: 177 us
  Pallas kernels  176 us (99%)
    pallas_call x1, Pallas kernels, on_device(): pl.pallas_call(kernel, out_shape=(jax.ShapeDtypeStruct((TOK, D), BF), jax...  174 us

profile of v4, /device:TPU:1, one launch (start us, length us, event | category | flops | bytes accessed | tf_op | source)
XLA Modules:
  0.0 177.1 jit_solution(13958961908646960953)
XLA Ops:
  0.6 173.6 %routed_backward.1 = (bf16[128,2048]{1,0:T(8,128)(2,1)}, bf16[8,128]{1,0:T(8,128)(2,1)}, f32[512,768]{1,0:T(8,128)}, f32[512,384]{1,0:T(8,128)}) custom-call(bf16[128,2048]{1,0:T(8,128)(2,1)} %tok_hbm.1, bf16[128,2048]{1,0:T(8,128)(2,1)} %dy_hbm.1, s32[8,128]{1,0:T(8,128)} %bitcast.11, bf16[8,128]{1,0:T(8,128)(2,1)} %bitcast.12, bf16[2048,768]{1,0:T(8,128)(2,1)} %bitcast.7, ...), custom_call_target="tpu_custom_call" | custom-call | flops 15000000512 | bytes 10000000 | tf_op jit(solution)/shard_map/routed_backward/pallas_call | solution.py:619
  174.2 2.8 %results.1 = (bf16[128,2048]{1,0:T(8,128)(2,1)}, bf16[8,128]{1,0:T(8,128)(2,1)}, f32[512,768]{1,0:T(8,128)}, f32[512,384]{1,0:T(8,128)}) custom-call(bf16[128,2048]{1,0:T(8,128)(2,1)} %get-tuple-element.12.refs_0_, bf16[8,128]{1,0:T(8,128)(2,1)} %get-tuple-element.13.refs_1_, f32[512,768]{1,0:T(8,128)} %get-tuple-element.14.refs_2_, ...), custom_call_target="tpu_custom_call" | custom-call | tf_op jit(solution)/shard_map/results/pallas_call | solution.py:686

commit v5 on v4

--- a/solution.py
+++ b/solution.py
@@ -398,8 +398,8 @@
     qin[rows16(s * 16, 16), :] = qbuf[rows16(s * 16, 16), :]
 
     def send_pair(k):
+        send_back(5 - 2 * k)
         send_back(4 - 2 * k)
-        send_back(5 - 2 * k)
 
     loop(0, 2, send_pair)
     send_back(1)
@@ -520,15 +520,16 @@
         gall[z] = gq[0]
 
     def back_turn(k):
-        @pl.when(k < 3)
+        @pl.when(k == 0)
+        def _():
+            pass_on(6, sgn, k > 0)
+
+        pass_on(7 - 2 * k, -sgn, k > 0)
+
+        @pl.when((k == 1) | (k == 2))
         def _():
             pass_on(6 - 2 * k, sgn, k > 0)
-
-        pass_on(7 - 2 * k, -sgn, k > 0)
-
-        @pl.when(k < 2)
-        def _():
-            m = k
+            m = k - 1
             grad_copy(0, m, sgn).wait()
 
             def emit(a, b):

time: 177 us -> 174 us (0.983)
  Pallas kernels: 176 us -> 173 us
    pallas_call x1, Pallas kernels: 174 us -> 171 us  [on_device(): pl.pallas_call(kernel, out_shape=(jax.ShapeDtypeStruct((TOK, D), BF), jax...]
where the time goes in v5:
time: 174 us
  Pallas kernels  173 us (99%)
    pallas_call x1, Pallas kernels, on_device(): pl.pallas_call(kernel, out_shape=(jax.ShapeDtypeStruct((TOK, D), BF), jax...  171 us

profile of v5, /device:TPU:1, one launch (start us, length us, event | category | flops | bytes accessed | tf_op | source)
XLA Modules:
  0.0 174.2 jit_solution(10710617723879653353)
XLA Ops:
  0.6 170.6 %routed_backward.1 = (bf16[128,2048]{1,0:T(8,128)(2,1)}, bf16[8,128]{1,0:T(8,128)(2,1)}, f32[512,768]{1,0:T(8,128)}, f32[512,384]{1,0:T(8,128)}) custom-call(bf16[128,2048]{1,0:T(8,128)(2,1)} %tok_hbm.1, bf16[128,2048]{1,0:T(8,128)(2,1)} %dy_hbm.1, s32[8,128]{1,0:T(8,128)} %bitcast.11, bf16[8,128]{1,0:T(8,128)(2,1)} %bitcast.12, bf16[2048,768]{1,0:T(8,128)(2,1)} %bitcast.7, ...), custom_call_target="tpu_custom_call" | custom-call | flops 15000000512 | bytes 10000000 | tf_op jit(solution)/shard_map/routed_backward/pallas_call | solution.py:620
  171.2 2.8 %results.1 = (bf16[128,2048]{1,0:T(8,128)(2,1)}, bf16[8,128]{1,0:T(8,128)(2,1)}, f32[512,768]{1,0:T(8,128)}, f32[512,384]{1,0:T(8,128)}) custom-call(bf16[128,2048]{1,0:T(8,128)(2,1)} %get-tuple-element.12.refs_0_, bf16[8,128]{1,0:T(8,128)(2,1)} %get-tuple-element.13.refs_1_, f32[512,768]{1,0:T(8,128)} %get-tuple-element.14.refs_2_, ...), custom_call_target="tpu_custom_call" | custom-call | tf_op jit(solution)/shard_map/results/pallas_call | solution.py:687
